TPU v7x, 32 devices: a whole 2x2x4 slice. The times are simulated.
32 devices in a mesh: lat: 4 (over y, x), fld: 8 (over z, core).
Axes of the slice: x: 2, y: 2, z: 4, core: 2. Of those that a mesh axis runs over, the one named last changes fastest.
Arguments:
- patches: bfloat16 [64, 16, 32, 512], P('fld', 'lat'), may hold values from -6 to 6
- segment_ids: int32 [64, 16, 32], P('fld'), may hold values from 0 to 2, as said below
- gain_attn: float32 [512], replicated, may hold values from 0.25 to 1.75
- bias_attn: float32 [512], replicated, may hold values from -2 to 2
- w_qkv: bfloat16 [512, 1536], replicated, may hold values from -0.25 to 0.25
- w_proj: bfloat16 [512, 512], replicated, may hold values from -0.5 to 0.5
- gain_mlp: float32 [512], replicated, may hold values from 0.25 to 1.75
- bias_mlp: float32 [512], replicated, may hold values from -2 to 2
- w_hidden: bfloat16 [512, 2048], replicated, may hold values from -0.25 to 0.25
- w_output: bfloat16 [2048, 512], replicated, may hold values from -0.1875 to 0.1875
- cotangent: bfloat16 [64, 16, 32, 512], P('fld', 'lat'), may hold values from -6 to 6
Outputs:
- layer_out: bfloat16 [64, 16, 32, 512], P('fld', 'lat')
- patch_grad: float32 [64, 16, 32, 512], P('fld', 'lat')
- attn_gain_grad: float32 [512], replicated
- attn_bias_grad: float32 [512], replicated
- qkv_grad: float32 [512, 1536], replicated
- proj_grad: float32 [512, 512], replicated
- mlp_gain_grad: float32 [512], replicated
- mlp_bias_grad: float32 [512], replicated
- hidden_grad: float32 [512, 2048], replicated
- output_grad: float32 [2048, 512], replicated
Inputs may be any that keep to these rules, and one draw needn't show every extreme that they name: `segment_ids`: within a field the ids are the same in all 16 rows of a column and never fall from column 0 to column 31; column 0 holds 0 and the last column 2.
All inputs are finite; a program needn't handle non-finite values.
Results may differ from a plain program's by a relative error of at most 0.01.
Values may be sent and summed in bfloat16 or wider, within the bound.
A program may use at most 448 MiB of HBM per device.

v0:
```python
import jax
import jax.numpy as jnp
from jax import lax
from jax.sharding import PartitionSpec as P

HEADS = 16
HEAD_DIM = 32


epsilon = 1e-06
highest = lax.Precision.HIGHEST


def extended(block, sides, width):
    for axis, dim in sides:
        count = lax.axis_size(axis)
        forward = [(i, i + 1) for i in range(count - 1)]
        backward = [(target, source) for source, target in forward]
        low = lax.ppermute(
            lax.slice_in_dim(block, block.shape[dim] - width, None, axis=dim), axis, forward
        )
        high = lax.ppermute(lax.slice_in_dim(block, 0, width, axis=dim), axis, backward)
        block = jnp.concatenate([low, block, high], axis=dim)
    return block


def shifted(value, axis, by):
    devices = lax.axis_size(axis)
    pairs = [(i, i + by) for i in range(devices) if 0 <= i + by < devices]
    return lax.ppermute(value, axis, pairs)


def layer_norm(values, norm_gain, norm_bias):
    center = jnp.mean(values, axis=-1, keepdims=True)
    offsets = values - center
    variance = jnp.mean(offsets * offsets, axis=-1, keepdims=True)
    return offsets * lax.rsqrt(variance + epsilon) * norm_gain + norm_bias


def gelu_exact(values):
    return jax.nn.gelu(values, approximate=False)


def per_device(
    patches,
    segment_ids,
    gain_attn,
    bias_attn,
    w_qkv,
    w_proj,
    gain_mlp,
    bias_mlp,
    w_hidden,
    w_output,
    cotangent,
):
    fields, band_rows, columns, model_width = patches.shape
    score_scale = HEAD_DIM ** (-0.5)
    w_query = w_qkv[:, :model_width]
    w_keyval = w_qkv[:, model_width:]
    feature_head = lax.broadcasted_iota(jnp.int32, (model_width, HEADS), 0) // HEAD_DIM
    head_column = lax.broadcasted_iota(jnp.int32, (model_width, HEADS), 1)
    head_sum = (feature_head == head_column).astype(jnp.float32)
    head_spread = jnp.transpose(head_sum).astype(jnp.bfloat16)

    def collapse(product):
        return jnp.dot(product, head_sum, precision=highest, preferred_element_type=jnp.float32)

    def spread(weights_low):
        return jnp.dot(weights_low, head_spread, preferred_element_type=jnp.float32)

    inputs = patches.astype(jnp.float32)
    normed, norm_pull = jax.vjp(layer_norm, inputs, gain_attn, bias_attn)
    normed_low = normed.astype(jnp.bfloat16)
    queries = jnp.einsum(
        "frcd,de->frce", normed_low, w_query, preferred_element_type=jnp.float32
    ).astype(jnp.bfloat16)
    keyval = jnp.einsum(
        "frcd,de->frce", normed_low, w_keyval, preferred_element_type=jnp.float32
    ).astype(jnp.bfloat16)
    kv_padded = extended(keyval, (("lat", 1),), 1)
    label_pad = jnp.pad(segment_ids, ((0, 0), (1, 1), (0, 0)), constant_values=-1)
    label_band = lax.dynamic_slice_in_dim(
        label_pad, lax.axis_index("lat") * band_rows, band_rows + 2, 1
    )
    own_labels = label_band[:, 1 : band_rows + 1]
    queries_wide = queries.astype(jnp.float32)
    offsets_list = [(shift_row, offset) for shift_row in range(3) for offset in range(-4, 5)]

    def window_at(shift_row, offset):
        rows_block = kv_padded[:, shift_row : shift_row + band_rows]
        moved = jnp.roll(rows_block, -offset, axis=2)
        return (moved[..., :model_width], moved[..., model_width:])

    def allowed_at(shift_row, offset):
        label_rows = jnp.roll(label_band[:, shift_row : shift_row + band_rows], -offset, axis=2)
        return (own_labels == label_rows)[..., None]

    def score_at(shift_row, offset):
        key_at, unused = window_at(shift_row, offset)
        raw_scores = collapse(queries_wide * key_at.astype(jnp.float32))
        return jnp.where(allowed_at(shift_row, offset), raw_scores * score_scale, -1000000000.0)

    score_list = [score_at(shift_row, offset) for shift_row, offset in offsets_list]
    row_peak = score_list[0]
    for entry in score_list[1:]:
        row_peak = jnp.maximum(row_peak, entry)
    exp_list = [jnp.exp(entry - row_peak) for entry in score_list]
    row_total = exp_list[0]
    for entry in exp_list[1:]:
        row_total = row_total + entry
    log_total = row_peak + jnp.log(row_total)
    attention_list = [(entry / row_total).astype(jnp.bfloat16) for entry in exp_list]
    context = None
    for index, (shift_row, offset) in enumerate(offsets_list):
        unused, value_at = window_at(shift_row, offset)
        term = spread(attention_list[index]) * value_at.astype(jnp.float32)
        context = term if context is None else context + term
    context = context.astype(jnp.bfloat16)
    residual = inputs + jnp.einsum(
        "frcd,de->frce", context, w_proj, preferred_element_type=jnp.float32
    )
    normed_mlp, norm_mlp_pull = jax.vjp(layer_norm, residual, gain_mlp, bias_mlp)
    normed_mlp_low = normed_mlp.astype(jnp.bfloat16)
    hidden_pre = jnp.einsum(
        "frcd,de->frce", normed_mlp_low, w_hidden, preferred_element_type=jnp.float32
    )
    activated, gelu_pull = jax.vjp(gelu_exact, hidden_pre)
    activated_low = activated.astype(jnp.bfloat16)
    mlp_out = jnp.einsum(
        "frce,ed->frcd", activated_low, w_output, preferred_element_type=jnp.float32
    )
    layer_out = (residual + mlp_out).astype(jnp.bfloat16)
    output_grad = jnp.einsum(
        "frce,frcd->ed", activated_low, cotangent, preferred_element_type=jnp.float32
    )
    grad_activated = jnp.einsum(
        "frcd,ed->frce", cotangent, w_output, preferred_element_type=jnp.float32
    )
    grad_pre = gelu_pull(grad_activated)[0].astype(jnp.bfloat16)
    hidden_grad = jnp.einsum(
        "frcd,frce->de", normed_mlp_low, grad_pre, preferred_element_type=jnp.float32
    )
    grad_normed_mlp = jnp.einsum(
        "frce,de->frcd", grad_pre, w_hidden, preferred_element_type=jnp.float32
    )
    grad_residual, mlp_gain_grad, mlp_bias_grad = norm_mlp_pull(grad_normed_mlp)
    grad_residual = grad_residual + cotangent.astype(jnp.float32)
    grad_branch = grad_residual.astype(jnp.bfloat16)
    proj_grad = jnp.einsum(
        "frcd,frce->de", context, grad_branch, preferred_element_type=jnp.float32
    )
    grad_context = jnp.einsum(
        "frce,de->frcd", grad_branch, w_proj, preferred_element_type=jnp.float32
    )
    grad_context = grad_context.astype(jnp.bfloat16)
    grad_context_wide = grad_context.astype(jnp.float32)
    prob_list = []
    grad_att_list = []
    for shift_row, offset in offsets_list:
        unused, value_at = window_at(shift_row, offset)
        grad_att_list.append(collapse(grad_context_wide * value_at.astype(jnp.float32)))
        prob_list.append(jnp.exp(score_at(shift_row, offset) - log_total))
    weighted_sum = prob_list[0] * grad_att_list[0]
    for index in range(1, len(prob_list)):
        weighted_sum = weighted_sum + prob_list[index] * grad_att_list[index]
    grad_queries = None
    row_grads = []
    for shift_row in range(3):
        row_sum = None
        for offset in range(-4, 5):
            index = 9 * shift_row + offset + 4
            grad_raw = (
                prob_list[index] * (grad_att_list[index] - weighted_sum) * score_scale
            ).astype(jnp.bfloat16)
            key_at, unused = window_at(shift_row, offset)
            raw_wide = spread(grad_raw)
            query_term = raw_wide * key_at.astype(jnp.float32)
            grad_queries = query_term if grad_queries is None else grad_queries + query_term
            key_term = raw_wide * queries_wide
            value_term = spread(attention_list[index]) * grad_context_wide
            placed = jnp.roll(jnp.concatenate([key_term, value_term], axis=-1), offset, axis=2)
            row_sum = placed if row_sum is None else row_sum + placed
        row_grads.append(row_sum)
    grad_kv = row_grads[1]
    grad_kv = grad_kv.at[:, : band_rows - 1].add(row_grads[0][:, 1:])
    grad_kv = grad_kv.at[:, 1:].add(row_grads[2][:, : band_rows - 1])
    above_rim = row_grads[0][:, :1]
    below_rim = row_grads[2][:, band_rows - 1 :]
    from_upper = shifted(above_rim.astype(jnp.bfloat16), "lat", -1).astype(above_rim.dtype)
    from_lower = shifted(below_rim.astype(jnp.bfloat16), "lat", 1).astype(below_rim.dtype)
    grad_kv = grad_kv.at[:, :1].add(from_lower).at[:, band_rows - 1 :].add(from_upper)
    grad_query_low = grad_queries.astype(jnp.bfloat16)
    grad_kv_low = grad_kv.astype(jnp.bfloat16)
    qkv_grad = jnp.concatenate(
        [
            jnp.einsum(
                "frcd,frce->de", normed_low, grad_query_low, preferred_element_type=jnp.float32
            ),
            jnp.einsum(
                "frcd,frce->de", normed_low, grad_kv_low, preferred_element_type=jnp.float32
            ),
        ],
        axis=1,
    )
    grad_normed = jnp.einsum(
        "frce,de->frcd", grad_query_low, w_query, preferred_element_type=jnp.float32
    )
    grad_normed = grad_normed + jnp.einsum(
        "frce,de->frcd", grad_kv_low, w_keyval, preferred_element_type=jnp.float32
    )
    patch_part, attn_gain_grad, attn_bias_grad = norm_pull(grad_normed)
    patch_grad = grad_residual + patch_part
    (
        attn_gain_grad,
        attn_bias_grad,
        qkv_grad,
        proj_grad,
        mlp_gain_grad,
        mlp_bias_grad,
        hidden_grad,
        output_grad,
    ) = lax.psum(
        (
            attn_gain_grad,
            attn_bias_grad,
            qkv_grad,
            proj_grad,
            mlp_gain_grad,
            mlp_bias_grad,
            hidden_grad,
            output_grad,
        ),
        ("lat", "fld"),
    )
    return (
        layer_out,
        patch_grad,
        attn_gain_grad,
        attn_bias_grad,
        qkv_grad,
        proj_grad,
        mlp_gain_grad,
        mlp_bias_grad,
        hidden_grad,
        output_grad,
    )


def solution(mesh):
    return jax.shard_map(
        per_device,
        mesh=mesh,
        in_specs=(
            P("fld", "lat", None, None),
            P("fld", None, None),
            P(),
            P(),
            P(),
            P(),
            P(),
            P(),
            P(),
            P(),
            P("fld", "lat", None, None),
        ),
        out_specs=(
            P("fld", "lat", None, None),
            P("fld", "lat", None, None),
            P(),
            P(),
            P(),
            P(),
            P(),
            P(),
            P(),
            P(),
        ),
        check_vma=False,
    )
```

profile of v0, /device:TPU:1, one launch (start us, length us, event | category | flops | bytes accessed | tf_op | source)
XLA Modules:
  0.0 858.0 jit_solution(9662138014691421436)
XLA Ops:
  17.4 4.8 collective-permute-start
  34.1 2.9 fusion.229
  40.4 3.7 fusion.253
  45.6 3.3 fusion.126
  48.9 3.3 fusion.251
  53.7 4.1 fusion.125
  57.8 3.0 fusion.249
  60.9 2.9 fusion.245
  63.8 2.9 fusion.243
  66.7 2.9 fusion.241
  69.6 3.7 fusion.128
  119.5 3.5 add_add_fusion.3
  170.4 30.8 %fusion.118 = (bf16[8,4,32,512]{3,2,1,0:T(8,128)(2,1)}, f32[8,4,32,512]{3,2,1,0:T(8,128)}) fusion(f32[8,4,32,512]{3,2,1,0:T(8,128)} %fusion.345, f32[8,4,32,512]{3,2,1,0:T(8,128)} %fusion.344, f32[8,4,32,512]{3,2,1,0:T(8,128)} %fusion.343, f32[8,4,32,512]{3,2,1,0:T(8,128)} %fusion.342, f32[8,4,32,512]{3,2,1,0:T(8,128)} %fusion.341, ...), kind=kOutput, calls=%fused_computation.387 | convolution fusion | flops 100220928 | bytes 113119744 | tf_op jit(solution)/shard_map/dot_general | solution.py:70
  204.1 4.2 fusion.199
  208.3 19.8 %multiply_convert_fusion = (bf16[8,4,32,2048]{3,2,1,0:T(8,128)(2,1)}, f32[8,4,32,2048]{3,2,1,0:T(8,128)}) fusion(f32[8,4,32,2048]{3,2,1,0:T(8,128)S(1)} %get-tuple-element.282, u8[4,32,2048]{2,1,0:T(8,128)(4,1)S(1)} %get-tuple-element.59, u8[4,32,2048]{2,1,0:T(8,128)(4,1)S(1)} %get-tuple-element.58), kind=kLoop, calls=%fused_computation.150 | loop fusion | flops 146800640 | bytes 21495808 | tf_op jit(solution)/shard_map/convert_element_type | solution.py:129
  228.0 7.4 add_convert_fusion
  235.5 3.3 multiply_reduce_fusion
  243.3 24.2 %convert_multiply_fusion.4 = (f32[8,4,32,512]{3,2,1,0:T(8,128)}, f32[8,4,32,512]{3,2,1,0:T(8,128)}, f32[8,4,32,512]{3,2,1,0:T(8,128)}, f32[8,4,32,512]{3,2,1,0:T...) fusion(f32[8,4,32,512]{3,2,1,0:T(8,128)S(1)} %copy-done.65, ...), kind=kOutput, calls=%fused_computation.4 | convolution fusion | flops 547356672 | bytes 78118912 | tf_op jit(solution)/shard_map/frce,de->frcd/dot_general | solution.py:153
  297.2 2.7 fusion.176
  327.8 4.3 multiply_add_fusion
  377.8 4.6 convolution_bitcast_fusion.1
  382.4 13.4 %convert_multiply_fusion.8 = (f32[8,4,32,512]{3,2,1,0:T(8,128)}, f32[8,4,32,512]{3,2,1,0:T(8,128)}, f32[8,4,32,512]{3,2,1,0:T(8,128)}, f32[8,4,32,512]{3,2,1,0:T...) fusion(f32[8,4,32,512]{3,2,1,0:T(8,128)} %fusion.338, ...), kind=kLoop, calls=%fused_computation.8 | loop fusion | flops 5242880 | bytes 38797312 | tf_op jit(solution)/shard_map/mul | solution.py:181
  398.5 14.0 %convert_multiply_fusion.62 = (f32[8,4,32,512]{3,2,1,0:T(8,128)}, f32[8,4,32,512]{3,2,1,0:T(8,128)}, f32[8,4,32,512]{3,2,1,0:T(8,128)}, f32[8,4,32,512]{3,2,1,0:...) fusion(bf16[8,4,32,512]{3,2,1,0:T(8,128)(2,1)S(1)} %copy-done.7, ...), kind=kOutput, calls=%fused_computation.62 | convolution fusion | flops 22134784 | bytes 39064064 | tf_op jit(solution)/shard_map/dot_general | solution.py:70
  412.4 5.3 slice_maximum_fusion.3
  417.7 2.8 slice_maximum_fusion.2
  421.4 2.8 slice_maximum_fusion.1
  425.1 2.8 slice_maximum_fusion
  428.8 24.5 %convert_multiply_fusion.58 = (f32[8,4,32,512]{3,2,1,0:T(8,128)}, f32[8,4,32,512]{3,2,1,0:T(8,128)}, f32[8,4,32,512]{3,2,1,0:T(8,128)}, f32[8,4,32,512]{3,2,1,0:...) fusion(bf16[8,4,32,512]{3,2,1,0:T(8,128)(2,1)S(1)} %copy-done.7, ...), kind=kOutput, calls=%fused_computation.58 | convolution fusion | flops 26853376 | bytes 76812800 | tf_op jit(solution)/shard_map/dot_general | solution.py:70
  453.3 18.2 %fusion.7 = f32[8,4,32,1024]{3,2,1,0:T(8,128)} fusion(f32[8,4,32,512]{3,2,1,0:T(8,128)} %get-tuple-element.202, f32[8,4,32,512]{3,2,1,0:T(8,128)} %get-tuple-element.193, f32[8,4,32,512]{3,2,1,0:T(8,128)} %get-tuple-element.201, f32[8,4,32,512]{3,2,1,0:T(8,128)} %get-tuple-element.192, f32[8,4,32,512]{3,2,1,0:T(8,128)} %get-tuple-element.200, ...), kind=kLoop, calls=%fused_computation.165 | loop fusion | flops 30408704 | bytes 57409536 | tf_op jit(solution)/shard_map/add | solution.py:183
  473.7 8.3 collective-permute-start.2
  482.0 28.5 %fusion.91 = bf16[8,4,32,512]{3,2,1,0:T(8,128)(2,1)S(1)} fusion(f32[8,4,32,512]{3,2,1,0:T(8,128)} %fusion.373, f32[8,4,32,512]{3,2,1,0:T(8,128)} %fusion.372, f32[8,4,32,512]{3,2,1,0:T(8,128)} %fusion.371, f32[8,4,32,512]{3,2,1,0:T(8,128)} %fusion.370, f32[8,4,32,512]{3,2,1,0:T(8,128)} %get-tuple-element.286, f32[8,4,32,512]{3,2,1,0:T(8,128)} %fusion.368, ...), kind=kLoop, calls=%fused_computation.360 | loop fusion | flops 83361792 | bytes 112721920 | tf_op jit(solution)/shard_map/convert_element_type | solution.py:193
  513.9 4.4 convolution_bitcast_fusion
  518.3 2.8 slice_maximum_fusion.11
  522.0 2.8 slice_maximum_fusion.10
  525.6 2.8 slice_maximum_fusion.9
  529.3 2.8 slice_maximum_fusion.8
  533.0 2.8 slice_maximum_fusion.7
  536.5 2.8 slice_maximum_fusion.6
  540.2 2.8 slice_maximum_fusion.5
  546.4 16.2 %fusion.39 = f32[8,4,32,1024]{3,2,1,0:T(8,128)S(1)} fusion(f32[8,4,32,512]{3,2,1,0:T(8,128)} %get-tuple-element.176, f32[8,4,32,512]{3,2,1,0:T(8,128)} %get-tuple-element.158, f32[8,4,32,512]{3,2,1,0:T(8,128)} %get-tuple-element.175, f32[8,4,32,512]{3,2,1,0:T(8,128)} %get-tuple-element.157, f32[8,4,32,512]{3,2,1,0:T(8,128)} %get-tuple-element.174, ...), kind=kLoop, calls=%fused_computation.229 | loop fusion | flops 30408704 | bytes 57409536 | tf_op jit(solution)/shard_map/add | solution.py:183
  562.7 17.8 %fusion.23 = f32[8,4,32,1024]{3,2,1,0:T(8,128)} fusion(f32[8,4,32,512]{3,2,1,0:T(8,128)} %get-tuple-element.195, f32[8,4,32,512]{3,2,1,0:T(8,128)} %get-tuple-element.186, f32[8,4,32,512]{3,2,1,0:T(8,128)} %get-tuple-element.184, f32[8,4,32,512]{3,2,1,0:T(8,128)} %get-tuple-element.166, f32[8,4,32,512]{3,2,1,0:T(8,128)} %get-tuple-element.183, ...), kind=kLoop, calls=%fused_computation.197 | loop fusion | flops 30408704 | bytes 57409536 | tf_op jit(solution)/shard_map/add | solution.py:183
  580.5 2.9 fusion.55
  588.1 11.4 %collective-permute-done.3 = bf16[8,1,32,1024]{3,2,1,0:T(8,128)(2,1)S(1)} collective-permute-done((bf16[8,1,32,1024]{3,2,1,0:T(8,128)(2,1)S(1)}, bf16[8,1,32,1024]{3,2,1,0:T(8,128)(2,1)S(1)}, u32[]{:S(2)}, u32[]{:S(2)}) %collective-permute-start.3) | collective-permute-done | bytes 524320 | tf_op jit(solution)/shard_map/ppermute | solution.py:30
  605.3 6.3 add_convert_fusion.1
  615.3 43.2 %all-reduce.1 = (f32[512]{0:T(512)}, f32[512]{0:T(512)}, f32[512]{0:T(512)}, f32[512]{0:T(512)}) all-reduce(f32[512]{0:T(512)S(1)} %get-tuple-element.62, f32[512]{0:T(512)S(1)} %get-tuple-element.65, f32[512]{0:T(512)S(1)} %copy-done.237, f32[512]{0:T(512)S(1)} %copy-done.238), channel_id=1, replica_groups=mesh['lat'=4,'fld'=8] {'lat','fld'}, use_global_device_ids=true, to_apply=%region_9.10 | all-reduce | flops 2048 | bytes 16384 | tf_op jit(solution)/shard_map/psum | solution.py:223
  658.5 3.4 add_add_fusion.2
  661.9 177.4 %all-reduce.5.cloned.1.call-done = (f32[512,1536]{1,0:T(8,128)}, f32[512,512]{1,0:T(8,128)}, f32[512,2048]{1,0:T(8,128)}, f32[2048,512]{1,0:T(8,128)}) async-done(((f32[512,1536]{1,0:T(8,128)}, f32[512,512]{1,0:T(8,128)}, f32[512,2048]{1,0:T(8,128)}, f32[2048,512]{1,0:T(8,128)}), (f32[512,1536]{1,0:T(8,128)}, f32[512,512]{1,0:T(8,128)}, f32[512,2048]{1,0:T(8,128)}, ...) | async-done | bytes 12582928 | tf_op jit(solution)/shard_map/psum | solution.py:223
  839.2 3.9 copy.43
  (637 shorter events, 271.6 us)
Async XLA Ops:
  7.2 196.6 %copy-start = (bf16[512,2048]{1,0:T(8,128)(2,1)S(1)}, bf16[512,2048]{1,0:T(8,128)(2,1)}, u32[]{:S(2)}) copy-start(bf16[512,2048]{1,0:T(8,128)(2,1)} %param.27) | copy-start | bytes 6291460
  7.2 832.0 %all-reduce.5.cloned.1.call-start = ((), (), s32[]{:S(2)}) async-start(), calls=%async_computation | async-start | bytes 25165824 | tf_op jit(solution)/shard_map/psum | solution.py:223
  16.1 20.8 %collective-permute-start.1 = (bf16[8,1,32,1024]{3,2,1,0:T(8,128)(2,1)}, bf16[8,1,32,1024]{3,2,1,0:T(8,128)(2,1)S(1)}, u32[]{:S(2)}, u32[]{:S(2)}) collective-permute-start(bf16[8,1,32,1024]{3,2,1,0:T(8,128)(2,1)} %get-tuple-element.147), channel_id=1, source_target_pairs={{8,0},{16,8},{24,16},{9,1},{17,9},{25,17},{10,2},{18,10},{26,18},{... | collective-permute-start | bytes 1572872 | tf_op jit(solution)/shard_map/ppermute | solution.py:22
  17.4 19.5 %collective-permute-start = (bf16[8,1,32,1024]{3,2,1,0:T(8,128)(2,1)}, bf16[8,1,32,1024]{3,2,1,0:T(8,128)(2,1)S(1)}, u32[]{:S(2)}, u32[]{:S(2)}) collective-permute-start(bf16[8,1,32,1024]{3,2,1,0:T(8,128)(2,1)} %get-tuple-element.148), channel_id=1, source_target_pairs={{0,8},{8,16},{16,24},{1,9},{9,17},{17,25},{2,10},{10,18},{18,26},{... | collective-permute-start | bytes 1572872 | tf_op jit(solution)/shard_map/ppermute | solution.py:19
  34.1 85.4 %copy-start.6 = (bf16[8,4,32,512]{3,2,1,0:T(8,128)(2,1)}, bf16[8,4,32,512]{3,2,1,0:T(8,128)(2,1)S(1)}, u32[]{:S(2)}) copy-start(bf16[8,4,32,512]{3,2,1,0:T(8,128)(2,1)S(1)} %convolution_convert_fusion.2) | copy-start | bytes 3145732
  38.5 60.2 %copy-start.105 = (bf16[8,4,3,1024]{3,2,1,0:T(4,128)(2,1)}, bf16[8,4,3,1024]{3,2,1,0:T(4,128)(2,1)S(1)}, u32[]{:S(2)}) copy-start(bf16[8,4,3,1024]{3,2,1,0:T(4,128)(2,1)S(1)} %get-tuple-element.88) | copy-start | bytes 589828
  38.5 72.0 %copy-start.101 = (bf16[8,4,3,1024]{3,2,1,0:T(4,128)(2,1)}, bf16[8,4,3,1024]{3,2,1,0:T(4,128)(2,1)S(1)}, u32[]{:S(2)}) copy-start(bf16[8,4,3,1024]{3,2,1,0:T(4,128)(2,1)S(1)} %get-tuple-element.87) | copy-start | bytes 589828
  40.4 39.6 %copy-start.23 = (bf16[8,4,29,1024]{3,2,1,0:T(8,128)(2,1)}, bf16[8,4,29,1024]{3,2,1,0:T(8,128)(2,1)S(1)}, u32[]{:S(2)}) copy-start(bf16[8,4,29,1024]{3,2,1,0:T(8,128)(2,1)S(1)} %get-tuple-element.130) | copy-start | bytes 5701636
  40.4 51.4 %copy-start.21 = (bf16[8,4,29,1024]{3,2,1,0:T(8,128)(2,1)}, bf16[8,4,29,1024]{3,2,1,0:T(8,128)(2,1)S(1)}, u32[]{:S(2)}) copy-start(bf16[8,4,29,1024]{3,2,1,0:T(8,128)(2,1)S(1)} %get-tuple-element.129) | copy-start | bytes 5701636
  40.4 58.3 %copy-start.15 = (bf16[8,4,29,1024]{3,2,1,0:T(8,128)(2,1)}, bf16[8,4,29,1024]{3,2,1,0:T(8,128)(2,1)S(1)}, u32[]{:S(2)}) copy-start(bf16[8,4,29,1024]{3,2,1,0:T(8,128)(2,1)S(1)} %get-tuple-element.90) | copy-start | bytes 5701636
  40.4 70.1 %copy-start.13 = (bf16[8,4,29,1024]{3,2,1,0:T(8,128)(2,1)}, bf16[8,4,29,1024]{3,2,1,0:T(8,128)(2,1)S(1)}, u32[]{:S(2)}) copy-start(bf16[8,4,29,1024]{3,2,1,0:T(8,128)(2,1)S(1)} %get-tuple-element.89) | copy-start | bytes 5701636
  45.6 55.5 %copy-start.190 = (bf16[8,4,2,1024]{3,2,1,0:T(2,128)(2,1)}, bf16[8,4,2,1024]{3,2,1,0:T(2,128)(2,1)S(1)}, u32[]{:S(2)}) copy-start(bf16[8,4,2,1024]{3,2,1,0:T(2,128)(2,1)S(1)} %get-tuple-element.92) | copy-start | bytes 393220
  48.9 52.2 %copy-start.27 = (bf16[8,4,30,1024]{3,2,1,0:T(8,128)(2,1)}, bf16[8,4,30,1024]{3,2,1,0:T(8,128)(2,1)S(1)}, u32[]{:S(2)}) copy-start(bf16[8,4,30,1024]{3,2,1,0:T(8,128)(2,1)S(1)} %get-tuple-element.94) | copy-start | bytes 5898244
  48.9 59.4 %copy-start.25 = (bf16[8,4,30,1024]{3,2,1,0:T(8,128)(2,1)}, bf16[8,4,30,1024]{3,2,1,0:T(8,128)(2,1)S(1)}, u32[]{:S(2)}) copy-start(bf16[8,4,30,1024]{3,2,1,0:T(8,128)(2,1)S(1)} %get-tuple-element.93) | copy-start | bytes 5898244
  73.4 39.4 %copy-start.11 = (bf16[8,4,28,1024]{3,2,1,0:T(8,128)(2,1)}, bf16[8,4,28,1024]{3,2,1,0:T(8,128)(2,1)S(1)}, u32[]{:S(2)}) copy-start(bf16[8,4,28,1024]{3,2,1,0:T(8,128)(2,1)S(1)} %get-tuple-element.85) | copy-start | bytes 5505028
  74.2 38.6 %copy-start.98 = (bf16[8,4,4,1024]{3,2,1,0:T(4,128)(2,1)}, bf16[8,4,4,1024]{3,2,1,0:T(4,128)(2,1)S(1)}, u32[]{:S(2)}) copy-start(bf16[8,4,4,1024]{3,2,1,0:T(4,128)(2,1)S(1)} %get-tuple-element.83) | copy-start | bytes 786436
  77.6 76.4 %copy-start.147 = (f32[8,4,32,16]{2,3,1,0:T(8,128)}, f32[8,4,32,16]{2,3,1,0:T(8,128)S(1)}, u32[]{:S(2)}) copy-start(f32[8,4,32,16]{2,3,1,0:T(8,128)S(1)} %fusion.239) | copy-start | bytes 196612
  80.0 72.2 %copy-start.175 = (f32[8,4,32,16]{2,3,1,0:T(8,128)}, f32[8,4,32,16]{2,3,1,0:T(8,128)S(1)}, u32[]{:S(2)}) copy-start(f32[8,4,32,16]{2,3,1,0:T(8,128)S(1)} %fusion.237) | copy-start | bytes 196612
  82.3 68.0 %copy-start.173 = (f32[8,4,32,16]{2,3,1,0:T(8,128)}, f32[8,4,32,16]{2,3,1,0:T(8,128)S(1)}, u32[]{:S(2)}) copy-start(f32[8,4,32,16]{2,3,1,0:T(8,128)S(1)} %fusion.235) | copy-start | bytes 196612
  84.7 63.8 %copy-start.171 = (f32[8,4,32,16]{2,3,1,0:T(8,128)}, f32[8,4,32,16]{2,3,1,0:T(8,128)S(1)}, u32[]{:S(2)}) copy-start(f32[8,4,32,16]{2,3,1,0:T(8,128)S(1)} %fusion.233) | copy-start | bytes 196612
  87.1 59.6 %copy-start.169 = (f32[8,4,32,16]{2,3,1,0:T(8,128)}, f32[8,4,32,16]{2,3,1,0:T(8,128)S(1)}, u32[]{:S(2)}) copy-start(f32[8,4,32,16]{2,3,1,0:T(8,128)S(1)} %fusion.231) | copy-start | bytes 196612
  89.4 53.8 %copy-start.167 = (f32[8,4,32,16]{2,3,1,0:T(8,128)}, f32[8,4,32,16]{2,3,1,0:T(8,128)S(1)}, u32[]{:S(2)}) copy-start(f32[8,4,32,16]{2,3,1,0:T(8,128)S(1)} %fusion.228) | copy-start | bytes 196612
  91.8 49.5 %copy-start.165 = (f32[8,4,32,16]{2,3,1,0:T(8,128)}, f32[8,4,32,16]{2,3,1,0:T(8,128)S(1)}, u32[]{:S(2)}) copy-start(f32[8,4,32,16]{2,3,1,0:T(8,128)S(1)} %fusion.226) | copy-start | bytes 196612
  94.1 45.3 %copy-start.163 = (f32[8,4,32,16]{2,3,1,0:T(8,128)}, f32[8,4,32,16]{2,3,1,0:T(8,128)S(1)}, u32[]{:S(2)}) copy-start(f32[8,4,32,16]{2,3,1,0:T(8,128)S(1)} %fusion.224) | copy-start | bytes 196612
  96.3 41.3 %copy-start.161 = (f32[8,4,32,16]{2,3,1,0:T(8,128)}, f32[8,4,32,16]{2,3,1,0:T(8,128)S(1)}, u32[]{:S(2)}) copy-start(f32[8,4,32,16]{2,3,1,0:T(8,128)S(1)} %fusion.222) | copy-start | bytes 196612
  98.7 37.1 %copy-start.126 = (f32[8,4,32,16]{2,3,1,0:T(8,128)}, f32[8,4,32,16]{2,3,1,0:T(8,128)S(1)}, u32[]{:S(2)}) copy-start(f32[8,4,32,16]{2,3,1,0:T(8,128)S(1)} %fusion.220) | copy-start | bytes 196612
  101.1 33.0 %copy-start.153 = (f32[8,4,32,16]{2,3,1,0:T(8,128)}, f32[8,4,32,16]{2,3,1,0:T(8,128)S(1)}, u32[]{:S(2)}) copy-start(f32[8,4,32,16]{2,3,1,0:T(8,128)S(1)} %fusion.218) | copy-start | bytes 196612
  103.4 28.7 %copy-start.151 = (f32[8,4,32,16]{2,3,1,0:T(8,128)}, f32[8,4,32,16]{2,3,1,0:T(8,128)S(1)}, u32[]{:S(2)}) copy-start(f32[8,4,32,16]{2,3,1,0:T(8,128)S(1)} %fusion.216) | copy-start | bytes 196612
  117.2 44.0 %copy-start.94 = (f32[8,4,32,16]{2,3,1,0:T(8,128)}, f32[8,4,32,16]{2,3,1,0:T(8,128)S(1)}, u32[]{:S(2)}) copy-start(f32[8,4,32,16]{2,3,1,0:T(8,128)S(1)} %fusion.247) | copy-start | bytes 196612
  123.1 45.5 %copy-start.177 = (f32[8,4,32,16]{2,3,1,0:T(8,128)}, f32[8,4,32,16]{2,3,1,0:T(8,128)S(1)}, u32[]{:S(2)}) copy-start(f32[8,4,32,16]{2,3,1,0:T(8,128)S(1)} %get-tuple-element.277) | copy-start | bytes 196612
  170.3 30.8 %copy-start.9 = (bf16[8,4,32,512]{3,2,1,0:T(8,128)(2,1)S(1)}, bf16[8,4,32,512]{3,2,1,0:T(8,128)(2,1)}, u32[]{:S(2)}) copy-start(bf16[8,4,32,512]{3,2,1,0:T(8,128)(2,1)} %param.19) | copy-start | bytes 3145732
  203.3 35.6 %copy-start.57 = (f32[8,4,32,512]{3,2,1,0:T(8,128)}, f32[8,4,32,512]{3,2,1,0:T(8,128)S(1)}, u32[]{:S(2)}) copy-start(f32[8,4,32,512]{3,2,1,0:T(8,128)S(1)} %get-tuple-element.281) | copy-start | bytes 6291460
  203.4 35.5 %copy-start.220 = (f32[8,4,32]{2,1,0:T(4,128)}, f32[8,4,32]{2,1,0:T(4,128)S(1)}, u32[]{:S(2)}) copy-start(f32[8,4,32]{2,1,0:T(4,128)S(1)} %broadcast_multiply_fusion) | copy-start | bytes 12292
  204.1 34.8 %copy-start.228 = (f32[8,4,32]{2,1,0:T(4,128)}, f32[8,4,32]{2,1,0:T(4,128)S(1)}, u32[]{:S(2)}) copy-start(f32[8,4,32]{2,1,0:T(4,128)S(1)} %fusion.622) | copy-start | bytes 12292
  286.1 41.5 %copy-start.188 = (f32[8,4,32,16]{2,3,1,0:T(8,128)}, f32[8,4,32,16]{2,3,1,0:T(8,128)S(1)}, u32[]{:S(2)}) copy-start(f32[8,4,32,16]{2,3,1,0:T(8,128)S(1)} %fusion.182) | copy-start | bytes 196612
  332.6 95.2 %copy-start.60 = (f32[8,4,32,512]{3,2,1,0:T(8,128)}, f32[8,4,32,512]{3,2,1,0:T(8,128)S(1)}, u32[]{:S(2)}) copy-start(f32[8,4,32,512]{3,2,1,0:T(8,128)S(1)} %fusion.356) | copy-start | bytes 6291460
  453.2 28.7 %copy-start.104 = (bf16[8,4,3,1024]{3,2,1,0:T(4,128)(2,1)S(1)}, bf16[8,4,3,1024]{3,2,1,0:T(4,128)(2,1)}, u32[]{:S(2)}) copy-start(bf16[8,4,3,1024]{3,2,1,0:T(4,128)(2,1)} %copy-done.101) | copy-start | bytes 589828
  453.2 28.7 %copy-start.107 = (bf16[8,4,3,1024]{3,2,1,0:T(4,128)(2,1)S(1)}, bf16[8,4,3,1024]{3,2,1,0:T(4,128)(2,1)}, u32[]{:S(2)}) copy-start(bf16[8,4,3,1024]{3,2,1,0:T(4,128)(2,1)} %copy-done.105) | copy-start | bytes 589828
  453.3 28.7 %copy-start.110 = (bf16[8,4,3,1024]{3,2,1,0:T(4,128)(2,1)S(1)}, bf16[8,4,3,1024]{3,2,1,0:T(4,128)(2,1)}, u32[]{:S(2)}) copy-start(bf16[8,4,3,1024]{3,2,1,0:T(4,128)(2,1)} %copy-done.108) | copy-start | bytes 589828
  453.3 28.7 %copy-start.113 = (bf16[8,4,3,1024]{3,2,1,0:T(4,128)(2,1)S(1)}, bf16[8,4,3,1024]{3,2,1,0:T(4,128)(2,1)}, u32[]{:S(2)}) copy-start(bf16[8,4,3,1024]{3,2,1,0:T(4,128)(2,1)} %copy-done.111) | copy-start | bytes 589828
  453.3 28.7 %copy-start.192 = (bf16[8,4,2,1024]{3,2,1,0:T(2,128)(2,1)S(1)}, bf16[8,4,2,1024]{3,2,1,0:T(2,128)(2,1)}, u32[]{:S(2)}) copy-start(bf16[8,4,2,1024]{3,2,1,0:T(2,128)(2,1)} %copy-done.190) | copy-start | bytes 393220
  473.7 113.1 %collective-permute-start.2 = (bf16[8,1,32,1024]{3,2,1,0:T(8,128)(2,1)}, bf16[8,1,32,1024]{3,2,1,0:T(8,128)(2,1)}, u32[]{:S(2)}, u32[]{:S(2)}) collective-permute-start(bf16[8,1,32,1024]{3,2,1,0:T(8,128)(2,1)} %slice.2366), channel_id=1, source_target_pairs={{0,8},{8,16},{16,24},{1,9},{9,17},{17,25},{2,10},{10,18},{18,26},{... | collective-permute-start | bytes 1572872 | tf_op jit(solution)/shard_map/ppermute | solution.py:30
  482.0 28.6 %copy-start.10 = (bf16[8,4,32,512]{3,2,1,0:T(8,128)(2,1)S(1)}, bf16[8,4,32,512]{3,2,1,0:T(8,128)(2,1)}, u32[]{:S(2)}) copy-start(bf16[8,4,32,512]{3,2,1,0:T(8,128)(2,1)} %param.19) | copy-start | bytes 3145732
  482.0 28.6 %copy-start.218 = (f32[8,4,32]{2,1,0:T(4,128)S(1)}, f32[8,4,32]{2,1,0:T(4,128)}, u32[]{:S(2)}) copy-start(f32[8,4,32]{2,1,0:T(4,128)} %copy-done.217) | copy-start | bytes 12292
  482.0 28.6 %copy-start.224 = (f32[8,4,32]{2,1,0:T(4,128)S(1)}, f32[8,4,32]{2,1,0:T(4,128)}, u32[]{:S(2)}) copy-start(f32[8,4,32]{2,1,0:T(4,128)} %copy-done.223) | copy-start | bytes 12292
  482.0 28.6 %copy-start.234 = (f32[512]{0:T(512)S(1)}, f32[512]{0:T(512)}, u32[]{:S(2)}) copy-start(f32[512]{0:T(512)} %param.21) | copy-start | bytes 6148
  584.6 14.8 %collective-permute-start.3 = (bf16[8,1,32,1024]{3,2,1,0:T(8,128)(2,1)S(1)}, bf16[8,1,32,1024]{3,2,1,0:T(8,128)(2,1)S(1)}, u32[]{:S(2)}, u32[]{:S(2)}) collective-permute-start(bf16[8,1,32,1024]{3,2,1,0:T(8,128)(2,1)S(1)} %slice.2365), channel_id=1, source_target_pairs={{8,0},{16,8},{24,16},{9,1},{17,9},{25,17},{10,2},{18,10},{26,18},{... | collective-permute-start | bytes 1572872 | tf_op jit(solution)/shard_map/ppermute | solution.py:30
  614.0 44.5 %copy-start.227 = (f32[8,4,32]{2,1,0:T(4,128)S(1)}, f32[8,4,32]{2,1,0:T(4,128)}, u32[]{:S(2)}) copy-start(f32[8,4,32]{2,1,0:T(4,128)} %copy-done.226) | copy-start | bytes 12292
  (198 other events, 974.7 us)
Sparse Core Ops, SparseCore 0:
  603.8 235.3 all-reduce.4
where the time goes:
time: 863 us; the launch traced here: 858 us
  matrix products  361 us (42%)
  other arithmetic  189 us (22%)
  waiting for transfers between devices  189 us (22%)
  local copies, waits for them, and re-layouts  43.3 us (5%)
  blocking collectives  43.2 us (5%)
  between operations  17.4 us (2%)
  starting transfers between devices  15.6 us (2%)
    psum x1, waiting for transfers between devices, per_device(): lax.psum((attn_gain_grad, attn_bias_grad, qkv_grad, proj_grad, mlp_gain_g...  177 us
    dot_general x54, matrix products, spread(): return jnp.dot(weights_low, head_spread, preferred_element_type=jnp.float32)  161 us
    dot_general x54, matrix products, collapse(): jnp.dot(product, head_sum, precision=highest, preferred_element_type=jnp....  131 us
    add x3, other arithmetic, per_device(): row_sum = placed if row_sum is None else row_sum + placed  52.3 us
    psum x1, blocking collectives, per_device(): lax.psum((attn_gain_grad, attn_bias_grad, qkv_grad, proj_grad, mlp_gain_g...  43.2 us
    concatenate x12, other arithmetic, per_device(): jnp.concatenate([key_term, value_term], axis=-1)  35.5 us
    unnamed x486, local copies, waits for them, and re-layouts  33.7 us
    convert_element_type x1, other arithmetic, per_device(): grad_query_low = grad_queries.astype(jnp.bfloat16)  28.5 us
  transfers between devices with their start and end apart: 5, of which 2 were waited for; matrix products, arithmetic and copies ran while one was open for 15% of the time, Pallas kernels for 0%

commit v1 on v0

v1 whole, which is shorter than its diff:
```python
import functools
import math

import jax
import jax.numpy as jnp
from jax import lax
from jax.experimental import pallas as pl
from jax.experimental.pallas import tpu as pltpu
from jax.sharding import PartitionSpec as P

HEAD_DIM = 32
GROUP = 8
WIDE = GROUP * HEAD_DIM
SCALE = HEAD_DIM ** -0.5
LOG2E = math.log2(math.e)
EPS = 1e-6
REACH = 4
NEG = -1e30
CHUNK = 512
BF = jnp.bfloat16
F32 = jnp.float32
MESH = pl.DeviceIdType.MESH

NT = (((1,), (1,)), ((), ()))
TN = (((0,), (0,)), ((), ()))


def dot(a, b, dims=None):
    if dims is None:
        return jnp.dot(a, b, preferred_element_type=F32)
    return lax.dot_general(a, b, dims, preferred_element_type=F32)


def normalize(x):
    center = jnp.mean(x, axis=-1, keepdims=True)
    off = x - center
    rstd = lax.rsqrt(jnp.mean(off * off, axis=-1, keepdims=True) + EPS)
    return off * rstd, rstd


def norm_pull(e, gain, n, rstd):
    ge = e * gain
    a = jnp.mean(ge, axis=-1, keepdims=True)
    b = jnp.mean(ge * n, axis=-1, keepdims=True)
    return (ge - a - n * b) * rstd


def gelu_both(u):
    z = jnp.abs(u) * (1.0 / math.sqrt(2.0))
    t = 1.0 / (1.0 + 0.3275911 * z)
    ex = jnp.exp2((u * u) * (-0.5 * LOG2E))
    poly = t * (0.254829592 + t * (-0.284496736 + t * (1.421413741 + t * (-1.453152027 + t * 1.061405429))))
    half = 0.5 * poly * ex
    cdf = jnp.where(u < 0, half, 1.0 - half)
    return u * cdf, cdf + u * (ex * (1.0 / math.sqrt(2.0 * math.pi)))


def row_sums(x):
    return jnp.sum(x, axis=0, keepdims=True)


class Plan:
    def __init__(self, mesh, fields, rows, cols, width, ff):
        self.lats = mesh.shape["lat"]
        self.flds = mesh.shape["fld"]
        self.zs = self.flds // 2
        self.fields, self.rows, self.cols = fields, rows, cols
        self.tf = rows * cols
        self.tokens = fields * self.tf
        self.width, self.ff = width, ff
        self.chunks = ff // CHUNK
        unit = 16 * self.lats * self.flds
        pad = lambda n: -(-n // unit) * unit
        blocks = width // 128
        mlp = CHUNK * blocks + width * (CHUNK // 128)
        self.sizes = [pad(mlp)] * self.chunks + [pad(width * blocks)] + [pad(width * (3 * WIDE // 128))] * 2


def body(plan, *refs):
    pn = plan
    np_ = len(pn.sizes)
    (patches, seg, gain_a, bias_a, w_qkv, w_proj, gain_m, bias_m, w_hid, w_out, cot) = refs[:11]
    out_layer, out_patch, out_vec = refs[11:14]
    out_ag = refs[14 : 14 + np_]
    sc = list(refs[14 + np_ :])

    def take(n=None):
        if n is None:
            return sc.pop(0)
        got = sc[:n]
        del sc[:n]
        return got

    wq, wp, wh, wo = take(4)
    pb, cb, segv, halo = take(4)
    normed, qb, kv, pt, ctx, res, nm, acco, accg, act, gpre, gctx, dq, dacc, edge = take(15)
    hsend, hrecv, bm, bmf, biasb, vec, vrz, vrx, vrc = take(9)
    sb, rc, rx, rz, ag = take(np_), take(np_), take(np_), take(np_), take(np_)
    in_sem, out_sem, halo_s, halo_r, back_s, back_r, rs_s, rs_r, v_s, v_r = take(10)

    lat = lax.axis_index("lat")
    fld = lax.axis_index("fld")
    core = lax.rem(fld, 2)
    z = lax.div(fld, 2)
    L, Z = pn.lats, pn.zs
    FD, R, C, TF, T, D = pn.fields, pn.rows, pn.cols, pn.tf, pn.tokens, pn.width

    ins = [(patches, pb), (w_qkv, wq), (seg, segv), (w_proj, wp), (cot, cb), (w_hid, wh), (w_out, wo)]
    loads = [pltpu.make_async_copy(s, d, in_sem.at[i]) for i, (s, d) in enumerate(ins)]
    for c in loads:
        c.start()

    pair = (lat, fld + 1 - 2 * core)
    lat_peers = [(lax.rem(lat + k, L), fld) for k in range(1, L)]
    z_peers = [(lat, lax.rem(z + k, Z) * 2 + core) for k in range(1, Z)]
    barrier = pltpu.get_barrier_semaphore()
    everyone = [pair] + lat_peers + z_peers
    for d in everyone:
        pl.semaphore_signal(barrier, inc=1, device_id=d, device_id_type=MESH)
    pl.semaphore_wait(barrier, len(everyone))

    up, down = (lat - 1, fld), (lat + 1, fld)
    has_up, has_down = lat > 0, lat < L - 1

    def remote(src, dst, s, r, dev):
        return pltpu.make_async_remote_copy(
            src_ref=src, dst_ref=dst, send_sem=s, recv_sem=r, device_id=dev, device_id_type=MESH
        )

    def arrived(ref, sem):
        pltpu.make_async_copy(ref, ref, sem).wait()

    halo_up = remote(patches.at[:, pl.ds(0, C)], halo.at[1], halo_s.at[0], halo_r.at[1], up)
    halo_dn = remote(patches.at[:, pl.ds(TF - C, C)], halo.at[0], halo_s.at[1], halo_r.at[0], down)
    pl.when(has_up)(halo_up.start)
    pl.when(has_down)(halo_dn.start)

    def rows_of(p):
        n = pn.sizes[p]
        return n, n // 2, n // 2 // L, n // 2 // L // Z

    def at(i, n):
        return pl.ds(pl.multiple_of(i * n, 16), n)

    def rs_pair(p):
        n, h, s, w = rows_of(p)
        remote(sb[p].at[at(1 - core, h)], rc[p], rs_s.at[p, 0], rs_r.at[p, 0], pair).start()

    def rs_lat(p):
        n, h, s, w = rows_of(p)
        arrived(rc[p], rs_r.at[p, 0])
        mine = sb[p].at[at(core, h)]
        mine[...] = (mine[...].astype(F32) + rc[p][...].astype(F32)).astype(BF)
        for k, dev in enumerate(lat_peers):
            src = sb[p].at[pl.ds(pl.multiple_of(core * h + dev[0] * s, 16), s)]
            remote(src, rx[p].at[k], rs_s.at[p, 1], rs_r.at[p, 1], dev).start()

    def rs_z(p):
        n, h, s, w = rows_of(p)
        arrived(rx[p], rs_r.at[p, 1])
        base = core * h + lat * s
        mine = sb[p].at[pl.ds(pl.multiple_of(base, 16), s)]
        total = mine[...].astype(F32)
        for k in range(L - 1):
            total = total + rx[p][k].astype(F32)
        mine[...] = total.astype(BF)
        for k, dev in enumerate(z_peers):
            zi = lax.rem(z + k + 1, Z)
            src = sb[p].at[pl.ds(pl.multiple_of(base + zi * w, 16), w)]
            remote(src, rz[p].at[k], rs_s.at[p, 2], rs_r.at[p, 2], dev).start()

    def ag_z(p):
        n, h, s, w = rows_of(p)
        arrived(rz[p], rs_r.at[p, 2])
        spot = pl.ds(pl.multiple_of(core * h + lat * s + z * w, 16), w)
        total = sb[p][spot, :].astype(F32)
        for k in range(Z - 1):
            total = total + rz[p][k].astype(F32)
        ag[p][spot, :] = total.astype(BF)
        for dev in z_peers:
            remote(ag[p].at[spot], ag[p].at[spot], rs_s.at[p, 3], rs_r.at[p, 3], dev).start()

    def ag_lat(p):
        n, h, s, w = rows_of(p)
        arrived(ag[p].at[pl.ds(0, (Z - 1) * w)], rs_r.at[p, 3])
        spot = pl.ds(pl.multiple_of(core * h + lat * s, 16), s)
        for dev in lat_peers:
            remote(ag[p].at[spot], ag[p].at[spot], rs_s.at[p, 4], rs_r.at[p, 4], dev).start()

    def ag_pair(p):
        n, h, s, w = rows_of(p)
        arrived(ag[p].at[pl.ds(0, (L - 1) * s)], rs_r.at[p, 4])
        spot = at(core, h)
        remote(ag[p].at[spot], ag[p].at[spot], rs_s.at[p, 5], rs_r.at[p, 5], pair).start()

    def ag_out(p):
        n, h, s, w = rows_of(p)
        arrived(ag[p].at[pl.ds(0, h)], rs_r.at[p, 5])
        pltpu.make_async_copy(ag[p], out_ag[p], out_sem.at[2 + p]).start()

    def finish(p):
        n, h, s, w = rows_of(p)
        for i, m in enumerate((h, (L - 1) * s, (Z - 1) * w, (Z - 1) * w, (L - 1) * s, h)):
            arrived(sb[p].at[pl.ds(0, m)], rs_s.at[p, i])
        pltpu.make_async_copy(ag[p], out_ag[p], out_sem.at[2 + p]).wait()

    stages = (rs_pair, rs_lat, rs_z, ag_z, ag_lat, ag_pair, ag_out)

    def put(p, start, value):
        rows, lanes = value.shape
        low = value.astype(BF)
        for j in range(lanes // 128):
            sb[p][start + j * rows : start + (j + 1) * rows, :] = low[:, j * 128 : (j + 1) * 128]

    rid = lax.broadcasted_iota(jnp.int32, (WIDE, WIDE), 0) // HEAD_DIM
    cid = lax.broadcasted_iota(jnp.int32, (WIDE, WIDE), 1) // HEAD_DIM
    same = jnp.where(rid == cid, 1.0, 0.0)
    bm[...] = same.astype(BF)
    bmf[...] = same

    ga, ba = gain_a[...].reshape(1, D), bias_a[...].reshape(1, D)
    gm, bmlp = gain_m[...].reshape(1, D), bias_m[...].reshape(1, D)
    loads[0].wait()

    def norm_one(f, carry):
        n, _ = normalize(pb[f].astype(F32))
        normed[pl.ds(pl.multiple_of(f * TF, TF), TF), :] = (n * ga + ba).astype(BF)
        return carry

    lax.fori_loop(0, FD, norm_one, 0)
    loads[1].wait()
    qb[...] = dot(normed[...], wq[:, :D]).astype(BF)
    for j in range(2):
        part = dot(normed[...], wq[:, (j + 1) * D : (j + 2) * D]).astype(BF)
        kv[:, C : C + TF, j * D : (j + 1) * D] = part.reshape(FD, TF, D)

    loads[2].wait()
    kcol = lax.broadcasted_iota(jnp.int32, (C, WIDE), 0)
    qcol = lax.rem(lax.broadcasted_iota(jnp.int32, (C, WIDE), 1), C)
    away = jnp.abs(kcol - qcol)
    near = jnp.minimum(away, C - away) <= REACH
    diag = lax.broadcasted_iota(jnp.int32, (C, C), 0) == lax.broadcasted_iota(jnp.int32, (C, C), 1)
    for f in range(FD):
        line = segv[f, 0:1, :].astype(F32)
        across = jnp.concatenate([line] * GROUP, axis=1)
        along = jnp.sum(jnp.where(diag, line, 0.0), axis=1, keepdims=True)
        biasb[f] = jnp.where(jnp.logical_and(near, along == across), 0.0, NEG)
    pole_top = jnp.where(has_up, 0.0, NEG)
    pole_bottom = jnp.where(has_down, 0.0, NEG)

    for side, ok, copy in ((0, has_up, halo_dn), (1, has_down, halo_up)):
        pl.when(ok)(copy.wait_recv)

        @pl.when(jnp.logical_not(ok))
        def _():
            halo[side] = jnp.zeros((FD, C, D), BF)

        n, _unused = normalize(halo[side].reshape(FD * C, D).astype(F32))
        low = (n * ga + ba).astype(BF)
        edge_kv = dot(low, wq[:, D:]).astype(BF).reshape(FD, C, 2 * D)
        start = 0 if side == 0 else TF + C
        kv[:, start : start + C, :] = edge_kv

    def diagonal(o):
        o = o * bmf[...]
        total = o[0:HEAD_DIM]
        for h in range(1, GROUP):
            total = total + o[h * HEAD_DIM : (h + 1) * HEAD_DIM]
        return total

    def widened(q):
        return jnp.concatenate([q] * GROUP, axis=0) * bm[...]

    def attend(f, carry):
        bias = biasb[f]
        for g in range(2):
            lanes = slice(g * WIDE, (g + 1) * WIDE)
            vlanes = slice(D + g * WIDE, D + (g + 1) * WIDE)
            for r in range(R):
                tok = pl.ds(pl.multiple_of(f * TF + r * C, C), C)
                win = slice(r * C, (r + 3) * C)
                s = dot(kv[f, win, lanes], widened(qb[tok, lanes]), NT)
                top = bias + pole_top if r == 0 else bias
                low = bias + pole_bottom if r == R - 1 else bias
                s = s + jnp.concatenate([top, bias, low], axis=0)
                m = jnp.max(s, axis=0, keepdims=True)
                p = jnp.exp2((s - m) * (SCALE * LOG2E))
                p = (p * (1.0 / row_sums(p))).astype(BF)
                pt[f, g * R + r] = p
                ctx[tok, lanes] = diagonal(dot(p, kv[f, win, vlanes], TN)).astype(BF)
        return carry

    lax.fori_loop(0, FD, attend, 0)

    loads[3].wait()
    res[...] = pb[...].reshape(T, D).astype(F32) + dot(ctx[...], wp[...])

    def norm_two(f, carry):
        tok = pl.ds(pl.multiple_of(f * TF, TF), TF)
        n, _ = normalize(res[tok, :])
        nm[tok, :] = (n * gm + bmlp).astype(BF)
        return carry

    lax.fori_loop(0, FD, norm_two, 0)

    for i in (4, 5, 6):
        loads[i].wait()
    tile = min(256, T)
    for c in range(pn.chunks):
        cs = slice(c * CHUNK, (c + 1) * CHUNK)

        def mlp_tile(t, carry, c=c, cs=cs):
            tok = pl.ds(pl.multiple_of(t * tile, tile), tile)
            hidden = dot(nm[tok, :], wh[:, cs])
            back = dot(cb[tok, :], wo[cs, :], NT)
            a, da = gelu_both(hidden)
            a = a.astype(BF)
            gp = (da * back).astype(BF)
            act[tok, :] = a
            gpre[tok, :] = gp
            fwd = dot(a, wo[cs, :])
            bwd = dot(gp, wh[:, cs], NT)
            if c == 0:
                acco[tok, :] = fwd
                accg[tok, :] = bwd
            else:
                acco[tok, :] += fwd
                accg[tok, :] += bwd
            return carry

        lax.fori_loop(0, T // tile, mlp_tile, 0)
        put(c, 0, dot(act[...], cb[...], TN))
        put(c, CHUNK * (D // 128), dot(nm[...], gpre[...], TN))
        for back in range(min(c + 1, 4)):
            stages[back](c - back)

    zero = jnp.zeros((1, D), F32)

    def mlp_end(f, carry):
        dg, db = carry
        tok = pl.ds(pl.multiple_of(f * TF, TF), TF)
        x = res[tok, :]
        act[tok, :] = (x + acco[tok, :]).astype(BF)
        n, rstd = normalize(x)
        e = accg[tok, :]
        gr = cb[tok, :].astype(F32) + norm_pull(e, gm, n, rstd)
        res[tok, :] = gr
        gpre[tok, :] = gr.astype(BF)
        return dg + row_sums(e * n), db + row_sums(e)

    mlp_gain, mlp_bias = lax.fori_loop(0, FD, mlp_end, (zero, zero))
    layer_copy = pltpu.make_async_copy(act, out_layer, out_sem.at[0])
    layer_copy.start()
    pj = pn.chunks
    put(pj, 0, dot(ctx[...], gpre[...], TN))
    gctx[...] = dot(gpre[...], wp[...], NT).astype(BF)

    todo = {}
    order = []
    nc = pn.chunks
    for step in range(1, 8):
        line = []
        if step == 1:
            line.append((0, pj))
        for p in range(nc):
            st = step + nc - 1 - p
            if st < 7:
                line.append((st, p))
        if 2 <= step:
            line.append((step - 1, pj))
        order.append(line)

    def run(line):
        for st, p in line:
            stages[st](p)

    def back_group(g, hooks):
        lanes = slice(g * WIDE, (g + 1) * WIDE)
        vlanes = slice(D + g * WIDE, D + (g + 1) * WIDE)

        def back_field(f, carry):
            for when, line in hooks:
                pl.when(f == when)(functools.partial(run, line))
            dacc[...] = jnp.zeros_like(dacc)
            for r in range(R):
                tok = pl.ds(pl.multiple_of(f * TF + r * C, C), C)
                win = slice(r * C, (r + 3) * C)
                qd = widened(qb[tok, lanes])
                dod = widened(gctx[tok, lanes])
                k = kv[f, win, lanes]
                p = pt[f, g * R + r]
                dp = dot(kv[f, win, vlanes], dod, NT)
                wide = p.astype(F32)
                pd = wide * dp
                ds = ((pd - wide * row_sums(pd)) * SCALE).astype(BF)
                dq[g, tok, 0:WIDE] = diagonal(dot(ds, k, TN)).astype(BF)
                dacc[win, 0:WIDE] += dot(ds, qd)
                dacc[win, WIDE:] += dot(p, dod)
            hsend[g, 0, f] = dacc[0:C, :].astype(BF)
            hsend[g, 1, f] = dacc[TF + C :, :].astype(BF)
            edge[0, f] = dacc[C : 2 * C, :]
            edge[1, f] = dacc[TF : TF + C, :]
            if R > 2:
                mid = pl.ds(pl.multiple_of(f * TF + C, C), TF - 2 * C)
                dq[g, mid, WIDE:] = dacc[2 * C : TF, :].astype(BF)
            return carry

        lax.fori_loop(0, FD, back_field, 0)
        to_up = remote(hsend.at[g, 0], hrecv.at[g, 1], back_s.at[g, 0], back_r.at[g, 1], up)
        to_dn = remote(hsend.at[g, 1], hrecv.at[g, 0], back_s.at[g, 1], back_r.at[g, 0], down)
        pl.when(has_up)(to_up.start)
        pl.when(has_down)(to_dn.start)
        return to_up, to_dn

    def back_edges(g, to_up, to_dn):
        pl.when(has_up)(to_dn.wait_recv)
        pl.when(has_down)(to_up.wait_recv)
        for side, ok, row in ((0, has_up, 0), (1, has_down, R - 1)):

            def add(f, carry, side=side, ok=ok, row=row):
                tok = pl.ds(pl.multiple_of(f * TF + row * C, C), C)
                more = jnp.where(ok, hrecv[g, side, f].astype(F32), 0.0)
                dq[g, tok, WIDE:] = (edge[side, f] + more).astype(BF)
                return carry

            lax.fori_loop(0, FD, add, 0)

    half = FD // 2
    copies = []
    for g in range(2):
        if g == 0:
            hooks = [(0, order[0]), (half, order[1])]
        else:
            hooks = [(0, order[3]), (half, order[4])]
        pairs = back_group(g, hooks)
        copies += pairs
        back_edges(g, *pairs)
        put(pj + 1 + g, 0, dot(normed[...], dq[g], TN))
        if g == 0:
            run(order[2])
            rs_pair(pj + 1)
            rs_lat(pj + 1)
        else:
            rs_pair(pj + 2)
            run(order[5])
            rs_z(pj + 1)
            rs_lat(pj + 2)

    def last_tile(f, carry):
        dg, db = carry
        tok = pl.ds(pl.multiple_of(f * TF, TF), TF)
        e = None
        for g in range(2):
            for j in range(3):
                w = wq[:, j * D + g * WIDE : j * D + (g + 1) * WIDE]
                term = dot(dq[g, tok, j * WIDE : (j + 1) * WIDE], w, NT)
                e = term if e is None else e + term
        n, rstd = normalize(pb[f].astype(F32))
        acco[tok, :] = res[tok, :] + norm_pull(e, ga, n, rstd)
        return dg + row_sums(e * n), db + row_sums(e)

    attn_gain, attn_bias = lax.fori_loop(0, FD, last_tile, (zero, zero))
    patch_copy = pltpu.make_async_copy(acco, out_patch, out_sem.at[1])
    patch_copy.start()
    vec[...] = jnp.concatenate([attn_gain, attn_bias, mlp_gain, mlp_bias, zero, zero, zero, zero], axis=0)

    def vec_send(buf, slot, peers, i):
        buf[slot] = vec[...]
        for dev in peers:
            remote(vec, buf.at[slot], v_s.at[i], v_r.at[i], dev).start()

    def vec_sum(buf, count, i):
        arrived(buf.at[pl.ds(0, count - 1)], v_r.at[i])
        arrived(buf.at[pl.ds(0, count - 1)], v_s.at[i])
        total = buf[0]
        for k in range(1, count):
            total = total + buf[k]
        vec[...] = total

    vec_send(vrz, z, z_peers, 0)
    run(order[6])
    ag_z(pj + 1)
    rs_z(pj + 2)
    vec_sum(vrz, Z, 0)
    vec_send(vrx, lat, lat_peers, 1)
    ag_lat(pj + 1)
    ag_z(pj + 2)
    vec_sum(vrx, L, 1)
    vec_send(vrc, core, [pair], 2)
    ag_pair(pj + 1)
    ag_lat(pj + 2)
    vec_sum(vrc, 2, 2)
    ag_out(pj + 1)
    ag_pair(pj + 2)
    vec_copy = pltpu.make_async_copy(vec, out_vec, in_sem.at[0])
    vec_copy.start()
    ag_out(pj + 2)

    pl.when(has_up)(halo_up.wait_send)
    pl.when(has_down)(halo_dn.wait_send)
    for to_up, to_dn in (copies[0:2], copies[2:4]):
        pl.when(has_up)(to_up.wait_send)
        pl.when(has_down)(to_dn.wait_send)
    layer_copy.wait()
    patch_copy.wait()
    vec_copy.wait()
    for p in range(np_):
        finish(p)


def widen(plan, *refs):
    pn = plan
    np_ = len(pn.sizes)
    ag, vec, layer, patch = refs[:np_], refs[np_], refs[np_ + 1], refs[np_ + 2]
    o_layer, o_patch, o_ag, o_ab, o_qkv, o_proj, o_mg, o_mb, o_hid, o_out = refs[np_ + 3 : np_ + 13]
    sc = list(refs[np_ + 13 :])
    low, wide = sc[:np_], sc[np_ : 2 * np_]
    in_sem, out_sem, pass_sem = sc[2 * np_ :]
    D = pn.width
    loads = [pltpu.make_async_copy(ag[p], low[p], in_sem.at[p]) for p in range(np_)]
    for c in loads:
        c.start()
    through = [
        pltpu.make_async_copy(layer, o_layer, pass_sem.at[0]),
        pltpu.make_async_copy(patch, o_patch, pass_sem.at[1]),
    ]
    for c in through:
        c.start()
    for i, o in enumerate((o_ag, o_ab, o_mg, o_mb)):
        o[...] = vec[i : i + 1, :].reshape(D)
    stores = []

    def store(src, dst):
        c = pltpu.make_async_copy(src, dst, out_sem.at[len(stores)])
        c.start()
        stores.append(c)

    def spread(p, start, rows, blocks, col):
        for j in range(blocks):
            wide[p][:, col + j * 128 : col + (j + 1) * 128] = low[p][
                start + j * rows : start + (j + 1) * rows, :
            ].astype(F32)

    for p in range(np_):
        loads[p].wait()
        if p < pn.chunks:
            spread(p, 0, CHUNK, D // 128, 0)
            store(wide[p].at[:, pl.ds(0, D)], o_out.at[pl.ds(p * CHUNK, CHUNK)])
            spread(p, CHUNK * (D // 128), D, CHUNK // 128, D)
            store(wide[p].at[:, pl.ds(D, CHUNK)], o_hid.at[:, pl.ds(p * CHUNK, CHUNK)])
        elif p == pn.chunks:
            spread(p, 0, D, D // 128, 0)
            store(wide[p], o_proj)
        else:
            g = p - pn.chunks - 1
            spread(p, 0, D, 3 * WIDE // 128, 0)
            for j in range(3):
                store(
                    wide[p].at[:, pl.ds(j * WIDE, WIDE)],
                    o_qkv.at[:, pl.ds(j * D + g * WIDE, WIDE)],
                )
    for c in stores + through:
        c.wait()


def per_device(mesh, patches, segment_ids, gain_attn, bias_attn, w_qkv, w_proj, gain_mlp, bias_mlp, w_hidden, w_output, cotangent):
    fields, rows, cols, width = patches.shape
    ff = w_hidden.shape[1]
    pn = Plan(mesh, fields, rows, cols, width, ff)
    np_ = len(pn.sizes)
    T, TF, D, C, R, FD = pn.tokens, pn.tf, width, cols, rows, fields
    L, Z = pn.lats, pn.zs
    anywhere = pl.BlockSpec(memory_space=pl.ANY)
    vmem = pl.BlockSpec(memory_space=pltpu.VMEM)
    V = pltpu.VMEM
    dma = pltpu.SemaphoreType.DMA
    scratch = [
        V((D, 3 * D), BF), V((D, D), BF), V((D, ff), BF), V((ff, D), BF),
        V((FD, TF, D), BF), V((T, D), BF), V(segment_ids.shape, jnp.int32), V((2, FD, C, D), BF),
        V((T, D), BF), V((T, D), BF), V((FD, TF + 2 * C, 2 * D), BF), V((FD, 2 * R, 3 * C, WIDE), BF),
        V((T, D), BF), V((T, D), F32), V((T, D), BF), V((T, D), F32), V((T, D), F32),
        V((T, CHUNK), BF), V((T, CHUNK), BF), V((T, D), BF), V((2, T, 3 * WIDE), BF),
        V((TF + 2 * C, 2 * WIDE), F32), V((2, FD, C, 2 * WIDE), F32),
        V((2, 2, FD, C, 2 * WIDE), BF), V((2, 2, FD, C, 2 * WIDE), BF),
        V((WIDE, WIDE), BF), V((WIDE, WIDE), F32), V((FD, C, WIDE), F32),
        V((8, D), F32), V((Z, 8, D), F32), V((L, 8, D), F32), V((2, 8, D), F32),
    ]
    scratch += [V((n, 128), BF) for n in pn.sizes]
    scratch += [V((n // 2, 128), BF) for n in pn.sizes]
    scratch += [V((L - 1, n // 2 // L, 128), BF) for n in pn.sizes]
    scratch += [V((Z - 1, n // 2 // L // Z, 128), BF) for n in pn.sizes]
    scratch += [V((n, 128), BF) for n in pn.sizes]
    scratch += [
        dma((7,)), dma((2 + np_,)), dma((2,)), dma((2,)), dma((2, 2)), dma((2, 2)),
        dma((np_, 6)), dma((np_, 6)), dma((3,)), dma((3,)),
    ]
    shape = jax.ShapeDtypeStruct
    outs = pl.pallas_call(
        functools.partial(body, pn),
        out_shape=[shape((T, D), BF), shape((T, D), F32), shape((8, D), F32)]
        + [shape((n, 128), BF) for n in pn.sizes],
        in_specs=[anywhere, anywhere, vmem, vmem, anywhere, anywhere, vmem, vmem, anywhere, anywhere, anywhere],
        out_specs=[anywhere] * (3 + np_),
        scratch_shapes=scratch,
        compiler_params=pltpu.CompilerParams(
            collective_id=0, has_side_effects=True, vmem_limit_bytes=62 * 2**20
        ),
        name="block",
    )(
        patches.reshape(FD, TF, D), segment_ids, gain_attn, bias_attn, w_qkv, w_proj, gain_mlp, bias_mlp,
        w_hidden, w_output, cotangent.reshape(T, D),
    )
    layer, patch, vec = outs[:3]
    ags = outs[3:]
    wides = [(D, D + CHUNK)] * pn.chunks + [(D, D)] + [(D, 3 * WIDE)] * 2
    final = pl.pallas_call(
        functools.partial(widen, pn),
        out_shape=[
            shape((T, D), BF), shape((T, D), F32), shape((D,), F32), shape((D,), F32), shape((D, 3 * D), F32),
            shape((D, D), F32), shape((D,), F32), shape((D,), F32), shape((D, ff), F32), shape((ff, D), F32),
        ],
        in_specs=[anywhere] * np_ + [vmem, anywhere, anywhere],
        out_specs=[anywhere, anywhere, vmem, vmem, anywhere, anywhere, vmem, vmem, anywhere, anywhere],
        scratch_shapes=[V((n, 128), BF) for n in pn.sizes]
        + [V(s, F32) for s in wides]
        + [dma((np_,)), dma((2 * pn.chunks + 7,)), dma((2,))],
        compiler_params=pltpu.CompilerParams(vmem_limit_bytes=40 * 2**20),
        name="widen",
    )(*ags, vec, layer, patch)
    block = (FD, R, C, D)
    return (final[0].reshape(block), final[1].reshape(block)) + tuple(final[2:])


def solution(mesh):
    band = P("fld", "lat", None, None)
    return jax.shard_map(
        functools.partial(per_device, mesh),
        mesh=mesh,
        in_specs=(band, P("fld", None, None)) + (P(),) * 8 + (band,),
        out_specs=(band, band) + (P(),) * 8,
        check_vma=False,
    )
```

time: 863 us -> 186 us (0.22)
  matrix products: 361 us -> 0 us
  other arithmetic: 189 us -> 0 us
  waiting for transfers between devices: 189 us -> 0 us
  Pallas kernels: 0 us -> 171 us
  blocking collectives: 43.2 us -> 0 us
  local copies, waits for them, and re-layouts: 43.3 us -> 11.7 us
  between operations: 17.4 us -> 0.85 us
  starting transfers between devices: 15.6 us -> 0 us
    dot_general x123 -> x0, matrix products: 361 us -> none  [the longest x54 161 us: spread(): return jnp.dot(weights_low, head_spread, preferred_element_type=jnp.float32)]
    psum x1 -> x0, waiting for transfers between devices: 177 us -> none  [per_device(): lax.psum((attn_gain_grad, attn_bias_grad, qkv_grad, proj_grad, mlp_gain_g...]
    pallas_call x0 -> x2, Pallas kernels: none -> 171 us  [the longest x1 164 us: per_device(): pl.pallas_call(functools.partial(body, pn), out_shape=[shape((T, D), BF),...]
    concatenate x21 -> x0, other arithmetic: 55.7 us -> none  [the longest x12 35.5 us: per_device(): jnp.concatenate([key_term, value_term], axis=-1)]
    add x4 -> x0, other arithmetic: 55.6 us -> none  [the longest x3 52.3 us: per_device(): row_sum = placed if row_sum is None else row_sum + placed]
    convert_element_type x3 -> x0, other arithmetic: 48.6 us -> none  [the longest x1 28.5 us: per_device(): grad_query_low = grad_queries.astype(jnp.bfloat16)]
    psum x1 -> x0, blocking collectives: 43.2 us -> none  [per_device(): lax.psum((attn_gain_grad, attn_bias_grad, qkv_grad, proj_grad, mlp_gain_g...]
    unnamed x486 -> x20, local copies, waits for them, and re-layouts: 33.7 us -> 11.7 us
  transfers between devices with their start and end apart: 5 -> 0, of which waited for: 2 -> 0; matrix products, arithmetic and copies ran while one was open for 15% -> 0% of each run, Pallas kernels for 0% -> 0%
where the time goes in v1:
time: 186 us; the launch traced here: 183 us
  Pallas kernels  171 us (92%)
  local copies, waits for them, and re-layouts  11.7 us (6%)
    pallas_call x1, Pallas kernels, per_device(): pl.pallas_call(functools.partial(body, pn), out_shape=[shape((T, D), BF),...  164 us
    unnamed x20, local copies, waits for them, and re-layouts  11.7 us
    pallas_call x1, Pallas kernels, per_device(): pl.pallas_call(functools.partial(widen, pn), out_shape=[shape((T, D), BF)...  6.71 us

profile of v1, /device:TPU:1, one launch (start us, length us, event | category | flops | bytes accessed | tf_op | source)
XLA Modules:
  0.0 183.4 jit_solution(11368653347884897602)
XLA Ops:
  0.6 164.1 %block.1 = (bf16[1024,512]{1,0:T(8,128)(2,1)}, f32[1024,512]{1,0:T(8,128)}, f32[8,512]{1,0:T(8,128)}, bf16[4096,128]{1,0:T(8,128)(2,1)}, bf16[4096,128]{1,0:T(8,...) custom-call(bf16[8,128,512]{2,1,0:T(8,128)(2,1)} %bitcast.4, ...), custom_call_target="tpu_custom_call" | custom-call | tf_op jit(solution)/shard_map/block/pallas_call | solution.py:598
  164.8 0.0 copy-start
  164.8 1.6 copy-done
  166.4 0.0 copy-start.1
  166.4 1.2 copy-done.1
  167.6 0.0 copy-start.2
  167.6 1.2 copy-done.2
  168.8 0.0 copy-start.3
  168.8 1.2 copy-done.3
  170.0 0.0 copy-start.4
  170.0 1.2 copy-done.4
  171.3 0.0 copy-start.5
  171.3 1.2 copy-done.5
  172.5 0.0 copy-start.6
  172.5 1.1 copy-done.6
  173.6 0.0 copy-start.7
  173.6 1.1 copy-done.7
  174.8 0.0 copy-start.8
  174.8 1.0 copy-done.8
  175.8 0.0 copy-start.9
  175.8 0.7 copy-done.9
  176.5 6.7 %widen.1 = (bf16[1024,512]{1,0:T(8,128)(2,1)}, f32[1024,512]{1,0:T(8,128)}, f32[512]{0:T(512)}, f32[512]{0:T(512)}, f32[512,1536]{1,0:T(8,128)}, /*index=5*/f32[...) custom-call(bf16[4096,128]{1,0:T(8,128)(2,1)S(1)} %copy-done.2, ...), custom_call_target="tpu_custom_call" | custom-call | tf_op jit(solution)/shard_map/widen/pallas_call | solution.py:616
Async XLA Ops:
  164.8 1.6 copy-start
  166.4 1.2 copy-start.1
  167.6 1.2 copy-start.2
  168.8 1.2 copy-start.3
  170.0 1.2 copy-start.4
  171.3 1.2 copy-start.5
  172.5 1.1 copy-start.6
  173.6 1.1 copy-start.7
  174.8 1.0 copy-start.8
  175.8 0.7 copy-start.9

commit v2 on v1

v2 whole, which is shorter than its diff:
```python
import functools
import math

import jax
import jax.numpy as jnp
from jax import lax
from jax.experimental import pallas as pl
from jax.experimental.pallas import tpu as pltpu
from jax.sharding import PartitionSpec as P

HEAD_DIM = 32
GROUP = 8
WIDE = GROUP * HEAD_DIM
SCALE = HEAD_DIM ** -0.5
LOG2E = math.log2(math.e)
EPS = 1e-6
REACH = 4
NEG = -1e30
CHUNK = 512
BF = jnp.bfloat16
F32 = jnp.float32
MESH = pl.DeviceIdType.MESH

NT = (((1,), (1,)), ((), ()))
TN = (((0,), (0,)), ((), ()))


def dot(a, b, dims=None):
    if dims is None:
        return jnp.dot(a, b, preferred_element_type=F32)
    return lax.dot_general(a, b, dims, preferred_element_type=F32)


def normalize(x):
    center = jnp.mean(x, axis=-1, keepdims=True)
    off = x - center
    rstd = lax.rsqrt(jnp.mean(off * off, axis=-1, keepdims=True) + EPS)
    return off * rstd, rstd


def norm_pull(e, gain, n, rstd):
    ge = e * gain
    a = jnp.mean(ge, axis=-1, keepdims=True)
    b = jnp.mean(ge * n, axis=-1, keepdims=True)
    return (ge - a - n * b) * rstd


def gelu_both(u):
    z = jnp.abs(u) * (1.0 / math.sqrt(2.0))
    t = 1.0 / (1.0 + 0.3275911 * z)
    ex = jnp.exp2((u * u) * (-0.5 * LOG2E))
    poly = t * (0.254829592 + t * (-0.284496736 + t * (1.421413741 + t * (-1.453152027 + t * 1.061405429))))
    half = 0.5 * poly * ex
    cdf = jnp.where(u < 0, half, 1.0 - half)
    return u * cdf, cdf + u * (ex * (1.0 / math.sqrt(2.0 * math.pi)))


def row_sums(x):
    return jnp.sum(x, axis=0, keepdims=True)


class Plan:
    def __init__(self, mesh, fields, rows, cols, width, ff):
        self.lats = mesh.shape["lat"]
        self.flds = mesh.shape["fld"]
        self.zs = self.flds // 2
        self.fields, self.rows, self.cols = fields, rows, cols
        self.tf = rows * cols
        self.tokens = fields * self.tf
        self.width, self.ff = width, ff
        self.chunks = ff // CHUNK
        self.size_of = {"core": 2, "x": 2, "y": self.lats // 2, "lat": self.lats, "z": self.zs}
        unit = 16 * self.lats * self.flds
        blocks = width // 128
        mlp = CHUNK * blocks + width * (CHUNK // 128)
        rows_needed = [mlp] * self.chunks + [width * blocks] + [width * (3 * WIDE // 128)] * 2
        self.sizes, self.subs = [], []
        for p, n in enumerate(rows_needed):
            n = -(-n // unit) * unit
            self.sizes.append(n)
            last = p >= len(rows_needed) - 1
            if last or n % (2 * unit):
                self.subs.append([(0, n, ("core", "lat", "z"))])
            else:
                self.subs.append([(0, n // 2, ("core", "x", "y", "z")), (n // 2, n // 2, ("core", "y", "x", "z"))])
        self.landing = []
        for subs in self.subs:
            total = 0
            for _, n, order in subs:
                for d in order:
                    n //= self.size_of[d]
                    total += n * (self.size_of[d] - 1)
            self.landing.append(total)
        self.n_subs = sum(len(s) for s in self.subs)


def body(plan, *refs):
    pn = plan
    np_ = len(pn.sizes)
    (patches, seg, gain_a, bias_a, w_qkv, w_proj, gain_m, bias_m, w_hid, w_out, cot) = refs[:11]
    out_layer, out_patch, out_vec = refs[11:14]
    out_ag = refs[14 : 14 + np_]
    sc = list(refs[14 + np_ :])

    def take(n):
        got = sc[:n]
        del sc[:n]
        return got

    wq, wp, wh, wo = take(4)
    pb, cb, segv, halo = take(4)
    normed, qb, kv, pt, ctx, res, nm, gres, act, gpre, gctx, dq, dacc, edge = take(14)
    hq, hg, lse, hlse, dst, hdst = take(6)
    bm, bmf, biasb, vec, vrz, vrx, vrc = take(7)
    sb, rb, ag = take(np_), take(np_), take(np_)
    in_sem, out_sem, halo_s, halo_r, back_s, back_r, rs_s, rs_r, v_s, v_r = take(10)

    lat = lax.axis_index("lat")
    fld = lax.axis_index("fld")
    core = lax.rem(fld, 2)
    z = lax.div(fld, 2)
    x = lax.rem(lat, 2)
    y = lax.div(lat, 2)
    L, Z, Y = pn.lats, pn.zs, pn.lats // 2
    FD, R, C, TF, T, D, FF = pn.fields, pn.rows, pn.cols, pn.tf, pn.tokens, pn.width, pn.ff

    ins = [(patches, pb), (w_qkv, wq), (seg, segv), (w_proj, wp), (cot, cb), (w_hid, wh), (w_out, wo)]
    loads = [pltpu.make_async_copy(s, d, in_sem.at[i]) for i, (s, d) in enumerate(ins)]
    for c in loads:
        c.start()

    me = {"core": core, "x": x, "y": y, "lat": lat, "z": z}

    def device(d, i):
        if d == "core":
            return lat, z * 2 + i
        if d == "x":
            return y * 2 + i, fld
        if d == "y":
            return i * 2 + x, fld
        if d == "lat":
            return i, fld
        return lat, i * 2 + core

    def peers(d):
        n = pn.size_of[d]
        places = [lax.rem(me[d] + k, n) for k in range(1, n)]
        return [(i, device(d, i)) for i in places]

    barrier = pltpu.get_barrier_semaphore()
    everyone = peers("core") + peers("lat") + peers("z")
    for _, dev in everyone:
        pl.semaphore_signal(barrier, inc=1, device_id=dev, device_id_type=MESH)
    pl.semaphore_wait(barrier, len(everyone))

    up, down = (lat - 1, fld), (lat + 1, fld)
    has_up, has_down = lat > 0, lat < L - 1

    def remote(src, dst, s, r, dev):
        return pltpu.make_async_remote_copy(
            src_ref=src, dst_ref=dst, send_sem=s, recv_sem=r, device_id=dev, device_id_type=MESH
        )

    def arrived(ref, sem):
        pltpu.make_async_copy(ref, ref, sem).wait()

    halo_up = remote(patches.at[:, pl.ds(0, C)], halo.at[1], halo_s.at[0], halo_r.at[1], up)
    halo_dn = remote(patches.at[:, pl.ds(TF - C, C)], halo.at[0], halo_s.at[1], halo_r.at[0], down)
    pl.when(has_up)(halo_up.start)
    pl.when(has_down)(halo_dn.start)

    def spot(off, n):
        return pl.ds(pl.multiple_of(off, 16), n)

    class Part:
        def __init__(self, p, number, start, n, order, land):
            self.p, self.number, self.order = p, number, order
            self.off, self.len, self.land = [start], [n], []
            for d in order:
                g = pn.size_of[d]
                n = n // g
                self.land.append(land)
                land += n * (g - 1)
                self.off.append(self.off[-1] + me[d] * n)
                self.len.append(n)
            self.end = land

        def moved(self, i):
            return self.len[i + 1] * (pn.size_of[self.order[i]] - 1)

        def scatter(self, i):
            n = self.len[i + 1]
            for k, (j, dev) in enumerate(peers(self.order[i])):
                src = sb[self.p].at[spot(self.off[i] + j * n, n)]
                dst = rb[self.p].at[pl.ds(self.land[i] + k * n, n)]
                remote(src, dst, rs_s.at[self.number, i], rs_r.at[self.number, i], dev).start()

        def add(self, i):
            n = self.len[i + 1]
            d = self.order[i]
            arrived(rb[self.p].at[pl.ds(self.land[i], self.moved(i))], rs_r.at[self.number, i])
            mine = spot(self.off[i + 1], n)
            total = sb[self.p][mine, :].astype(F32)
            for k in range(pn.size_of[d] - 1):
                total = total + rb[self.p][self.land[i] + k * n : self.land[i] + (k + 1) * n, :].astype(F32)
            to = ag if i == len(self.order) - 1 else sb
            to[self.p][mine, :] = total.astype(BF)

        def gather(self, i):
            s = 4 + i
            mine = ag[self.p].at[spot(self.off[i + 1], self.len[i + 1])]
            for _, dev in peers(self.order[i]):
                remote(mine, mine, rs_s.at[self.number, s], rs_r.at[self.number, s], dev).start()

        def gathered(self, i):
            arrived(ag[self.p].at[pl.ds(0, self.moved(i))], rs_r.at[self.number, 4 + i])

        def step(self, s):
            nd = len(self.order)
            if s < nd:
                if s > 0:
                    self.add(s - 1)
                self.scatter(s)
            elif s == nd:
                self.add(nd - 1)
                self.gather(nd - 1)
            else:
                self.gathered(2 * nd - s)
                if s < 2 * nd:
                    self.gather(2 * nd - 1 - s)

        def finish(self):
            for i in range(len(self.order)):
                for s in (i, 4 + i):
                    arrived(sb[self.p].at[pl.ds(0, self.moved(i))], rs_s.at[self.number, s])

    parts, number = [], 0
    for p in range(np_):
        mine, land = [], 0
        for start, n, order in pn.subs[p]:
            mine.append(Part(p, number, start, n, order, land))
            land = mine[-1].end
            number += 1
        parts.append(mine)
    reached = [0] * np_
    last_step = [2 * len(m[0].order) for m in parts]

    def hook(*pieces):
        steps = []
        for p in pieces:
            if reached[p] <= last_step[p]:
                steps.append((p, reached[p]))
                reached[p] += 1

        def run():
            for p, s in steps:
                for part in parts[p]:
                    part.step(s)
                if s == last_step[p]:
                    pltpu.make_async_copy(ag[p], out_ag[p], out_sem.at[2 + p]).start()

        return run

    def advance(*pieces):
        hook(*pieces)()

    def finish(p):
        for part in parts[p]:
            part.finish()
        pltpu.make_async_copy(ag[p], out_ag[p], out_sem.at[2 + p]).wait()

    def put(p, start, value):
        rows, lanes = value.shape
        low = value.astype(BF)
        for j in range(lanes // 128):
            sb[p][start + j * rows : start + (j + 1) * rows, :] = low[:, j * 128 : (j + 1) * 128]

    rid = lax.broadcasted_iota(jnp.int32, (WIDE, WIDE), 0) // HEAD_DIM
    cid = lax.broadcasted_iota(jnp.int32, (WIDE, WIDE), 1) // HEAD_DIM
    same = jnp.where(rid == cid, 1.0, 0.0)
    bm[...] = same.astype(BF)
    bmf[...] = same

    ga, ba = gain_a[...].reshape(1, D), bias_a[...].reshape(1, D)
    gm, bmlp = gain_m[...].reshape(1, D), bias_m[...].reshape(1, D)
    loads[0].wait()

    def norm_one(f, carry):
        n, _ = normalize(pb[f].astype(F32))
        normed[pl.ds(pl.multiple_of(f * TF, TF), TF), :] = (n * ga + ba).astype(BF)
        return carry

    lax.fori_loop(0, FD, norm_one, 0)
    loads[1].wait()
    qb[...] = dot(normed[...], wq[:, :D]).astype(BF)
    for j in range(2):
        part = dot(normed[...], wq[:, (j + 1) * D : (j + 2) * D]).astype(BF)
        kv[:, C : C + TF, j * D : (j + 1) * D] = part.reshape(FD, TF, D)

    loads[2].wait()
    kcol = lax.broadcasted_iota(jnp.int32, (C, WIDE), 0)
    qcol = lax.rem(lax.broadcasted_iota(jnp.int32, (C, WIDE), 1), C)
    away = jnp.abs(kcol - qcol)
    near = jnp.minimum(away, C - away) <= REACH
    diag = lax.broadcasted_iota(jnp.int32, (C, C), 0) == lax.broadcasted_iota(jnp.int32, (C, C), 1)
    for f in range(FD):
        line = segv[f, 0:1, :].astype(F32)
        across = jnp.concatenate([line] * GROUP, axis=1)
        along = jnp.sum(jnp.where(diag, line, 0.0), axis=1, keepdims=True)
        biasb[f] = jnp.where(jnp.logical_and(near, along == across), 0.0, NEG)
    pole_top = jnp.where(has_up, 0.0, NEG)
    pole_bottom = jnp.where(has_down, 0.0, NEG)

    def diagonal(o):
        o = o * bmf[...]
        total = o[0:HEAD_DIM]
        for h in range(1, GROUP):
            total = total + o[h * HEAD_DIM : (h + 1) * HEAD_DIM]
        return total

    def widened(q):
        return jnp.concatenate([q] * GROUP, axis=0) * bm[...]

    def attend(rows, f, carry):
        bias = biasb[f]
        for g in range(2):
            lanes = slice(g * WIDE, (g + 1) * WIDE)
            vlanes = slice(D + g * WIDE, D + (g + 1) * WIDE)
            for r in rows:
                tok = pl.ds(pl.multiple_of(f * TF + r * C, C), C)
                win = slice(r * C, (r + 3) * C)
                s = dot(kv[f, win, lanes], widened(qb[tok, lanes]), NT)
                top = bias + pole_top if r == 0 else bias
                low = bias + pole_bottom if r == R - 1 else bias
                s = s + jnp.concatenate([top, bias, low], axis=0)
                m = jnp.max(s, axis=0, keepdims=True)
                p = jnp.exp2((s - m) * (SCALE * LOG2E))
                total = row_sums(p)
                if r == 0 or r == R - 1:
                    lse[0 if r == 0 else 1, pl.ds(f * 2 + g, 1), :] = m * (SCALE * LOG2E) + jnp.log2(total)
                p = (p * (1.0 / total)).astype(BF)
                pt[f, g * R + r] = p
                ctx[tok, lanes] = diagonal(dot(p, kv[f, win, vlanes], TN)).astype(BF)
        return carry

    if R > 2:
        lax.fori_loop(0, FD, functools.partial(attend, range(1, R - 1)), 0)

    for side, ok, copy in ((0, has_up, halo_dn), (1, has_down, halo_up)):
        pl.when(ok)(copy.wait_recv)

        @pl.when(jnp.logical_not(ok))
        def _():
            halo[side] = jnp.zeros((FD, C, D), BF)

        n, _unused = normalize(halo[side].reshape(FD * C, D).astype(F32))
        low = (n * ga + ba).astype(BF)
        hq[side] = dot(low, wq[:, :D]).astype(BF)
        edge_kv = dot(low, wq[:, D:]).astype(BF).reshape(FD, C, 2 * D)
        start = 0 if side == 0 else TF + C
        kv[:, start : start + C, :] = edge_kv

    lax.fori_loop(0, FD, functools.partial(attend, (0, R - 1)), 0)

    loads[3].wait()
    per = max(1, 256 // TF)
    tile = per * TF

    def project(t, carry):
        tok = pl.ds(pl.multiple_of(t * tile, tile), tile)
        r = pb[pl.ds(t * per, per)].reshape(tile, D).astype(F32) + dot(ctx[tok, :], wp[...])
        res[tok, :] = r
        n, _ = normalize(r)
        nm[tok, :] = (n * gm + bmlp).astype(BF)
        return carry

    lax.fori_loop(0, T // tile, project, 0)

    for i in (4, 5, 6):
        loads[i].wait()
    mid = (T // tile) // 2
    mids = [(), (0,), (0, 1), (0, 1, 2)]
    ends = [(0,), (1,), (0, 2), (0, 1, 3)]
    for c in range(pn.chunks):
        cs = slice(c * CHUNK, (c + 1) * CHUNK)

        meanwhile = hook(*mids[c])

        def mlp_tile(t, carry, cs=cs, meanwhile=meanwhile):
            pl.when(t == mid)(meanwhile)
            tok = pl.ds(pl.multiple_of(t * tile, tile), tile)
            hidden = dot(nm[tok, :], wh[:, cs])
            back = dot(cb[tok, :], wo[cs, :], NT)
            a, da = gelu_both(hidden)
            act[tok, cs] = a.astype(BF)
            gpre[tok, cs] = (da * back).astype(BF)
            return carry

        lax.fori_loop(0, T // tile, mlp_tile, 0)
        put(c, 0, dot(act[:, cs], cb[...], TN))
        put(c, CHUNK * (D // 128), dot(nm[...], gpre[:, cs], TN))
        advance(*ends[c])

    zero = jnp.zeros((1, D), F32)

    def mlp_end(t, carry):
        dg, db = carry
        tok = pl.ds(pl.multiple_of(t * tile, tile), tile)
        e = dot(gpre[tok, :], wh[...], NT)
        n, rstd = normalize(res[tok, :])
        gr = cb[tok, :].astype(F32) + norm_pull(e, gm, n, rstd)
        gres[tok, :] = gr
        low = gr.astype(BF)
        nm[tok, :] = low
        gctx[pl.ds(t * per, per)] = dot(low, wp[...], NT).astype(BF).reshape(per, TF, D)
        return dg + row_sums(e * n), db + row_sums(e)

    mlp_gain, mlp_bias = lax.fori_loop(0, T // tile, mlp_end, (zero, zero))
    pj = pn.chunks
    g_up = remote(gctx.at[:, pl.ds(0, C)], hg.at[1], back_s.at[0], back_r.at[1], up)
    g_dn = remote(gctx.at[:, pl.ds(TF - C, C)], hg.at[0], back_s.at[1], back_r.at[0], down)
    l_up = remote(lse.at[0], hlse.at[1], back_s.at[2], back_r.at[3], up)
    l_dn = remote(lse.at[1], hlse.at[0], back_s.at[3], back_r.at[2], down)
    for to_up, to_dn in ((g_up, g_dn), (l_up, l_dn)):
        pl.when(has_up)(to_up.start)
        pl.when(has_down)(to_dn.start)
    advance(1, 2)
    put(pj, 0, dot(ctx[...], nm[...], TN))
    advance(0, 3, pj)

    def back_group(g, hooks):
        lanes = slice(g * WIDE, (g + 1) * WIDE)
        vlanes = slice(D + g * WIDE, D + (g + 1) * WIDE)

        def back_field(f, carry):
            for when, do in hooks.items():
                pl.when(f == when)(do)
            dacc[...] = jnp.zeros_like(dacc)
            for r in range(R):
                tok = pl.ds(pl.multiple_of(f * TF + r * C, C), C)
                win = slice(r * C, (r + 3) * C)
                qd = widened(qb[tok, lanes])
                dod = widened(gctx[f, r * C : (r + 1) * C, lanes])
                k = kv[f, win, lanes]
                p = pt[f, g * R + r]
                dp = dot(kv[f, win, vlanes], dod, NT)
                wide = p.astype(F32)
                pd = wide * dp
                total = row_sums(pd)
                if r == 0 or r == R - 1:
                    dst[g, 0 if r == 0 else 1, pl.ds(f, 1), :] = total
                ds = ((pd - wide * total) * SCALE).astype(BF)
                dq[g, tok, 0:WIDE] = diagonal(dot(ds, k, TN)).astype(BF)
                dacc[win, 0:WIDE] += dot(ds, qd)
                dacc[win, WIDE:] += dot(p, dod)
            edge[g, 0, f] = dacc[C : 2 * C, :]
            edge[g, 1, f] = dacc[TF : TF + C, :]
            if R > 2:
                inner = pl.ds(pl.multiple_of(f * TF + C, C), TF - 2 * C)
                dq[g, inner, WIDE:] = dacc[2 * C : TF, :].astype(BF)
            return carry

        lax.fori_loop(0, FD, back_field, 0)
        to_up = remote(dst.at[g, 0], hdst.at[g, 1], back_s.at[4 + 2 * g], back_r.at[5 + 2 * g], up)
        to_dn = remote(dst.at[g, 1], hdst.at[g, 0], back_s.at[5 + 2 * g], back_r.at[4 + 2 * g], down)
        pl.when(has_up)(to_up.start)
        pl.when(has_down)(to_dn.start)
        return to_up, to_dn

    def back_edges(g, sent):
        lanes = slice(g * WIDE, (g + 1) * WIDE)
        vlanes = slice(D + g * WIDE, D + (g + 1) * WIDE)
        for to_up, to_dn in sent:
            pl.when(has_up)(to_dn.wait_recv)
            pl.when(has_down)(to_up.wait_recv)

        def one(f, carry):
            for side, ok, row in ((0, has_up, 0), (1, has_down, R - 1)):
                tok = pl.ds(pl.multiple_of(f * TF + row * C, C), C)
                keys = slice((row + 1) * C, (row + 2) * C)
                qd = widened(hq[side, pl.ds(pl.multiple_of(f * C, C), C), lanes])
                dod = widened(hg[side, f, :, lanes])
                s = dot(kv[f, keys, lanes], qd, NT) + biasb[f]
                p = jnp.exp2(s * (SCALE * LOG2E) - hlse[side, pl.ds(f * 2 + g, 1), :])
                p = jnp.where(ok, p, 0.0)
                dp = dot(kv[f, keys, vlanes], dod, NT)
                ds = p * (dp - hdst[g, side, pl.ds(f, 1), :]) * SCALE
                ds = jnp.where(ok, ds, 0.0).astype(BF)
                dk = edge[g, side, f, :, 0:WIDE] + jnp.where(ok, dot(ds, qd), 0.0)
                dv = edge[g, side, f, :, WIDE:] + jnp.where(ok, dot(p.astype(BF), dod), 0.0)
                dq[g, tok, WIDE : 2 * WIDE] = dk.astype(BF)
                dq[g, tok, 2 * WIDE :] = dv.astype(BF)
            return carry

        lax.fori_loop(0, FD, one, 0)
        put(pj + 1 + g, 0, dot(normed[...], dq[g], TN))

    every = list(range(pj + 1))
    sent0 = back_group(0, {1: hook(1, 2), 3: hook(0, 3, pj), 5: hook(1, 2), 7: hook(0, 3, pj)})

    early = {0: hook(1, 2), 2: hook(0, 3, pj)}
    start_first = hook(pj + 1)

    def first_edges():
        back_edges(0, ((g_up, g_dn), (l_up, l_dn), sent0))
        start_first()

    sent1 = back_group(1, early | {4: first_edges, 5: hook(1, 2, pj + 1), 6: hook(3, pj), 7: hook(2, pj)})
    advance(3, pj + 1)
    back_edges(1, (sent1,))
    advance(pj + 2)
    advance(pj + 1, *every)

    def out_tile(t, carry):
        tok = pl.ds(pl.multiple_of(t * tile, tile), tile)
        nm[tok, :] = (res[tok, :] + dot(act[tok, :], wo[...])).astype(BF)
        return carry

    lax.fori_loop(0, T // tile, out_tile, 0)
    layer_copy = pltpu.make_async_copy(nm, out_layer, out_sem.at[0])
    layer_copy.start()
    advance(pj + 2)
    advance(pj + 1, *every)

    def last_tile(t, carry):
        dg, db = carry
        tok = pl.ds(pl.multiple_of(t * tile, tile), tile)
        e = None
        for g in range(2):
            for j in range(3):
                w = wq[:, j * D + g * WIDE : j * D + (g + 1) * WIDE]
                term = dot(dq[g, tok, j * WIDE : (j + 1) * WIDE], w, NT)
                e = term if e is None else e + term
        n, rstd = normalize(pb[pl.ds(t * per, per)].reshape(tile, D).astype(F32))
        gres[tok, :] += norm_pull(e, ga, n, rstd)
        return dg + row_sums(e * n), db + row_sums(e)

    attn_gain, attn_bias = lax.fori_loop(0, T // tile, last_tile, (zero, zero))
    patch_copy = pltpu.make_async_copy(gres, out_patch, out_sem.at[1])
    patch_copy.start()
    vec[...] = jnp.concatenate([attn_gain, attn_bias, mlp_gain, mlp_bias, zero, zero, zero, zero], axis=0)

    def vec_send(buf, d, i):
        buf[me[d]] = vec[...]
        for _, dev in peers(d):
            remote(vec, buf.at[me[d]], v_s.at[i], v_r.at[i], dev).start()

    def vec_sum(buf, d, i):
        count = pn.size_of[d]
        arrived(buf.at[pl.ds(0, count - 1)], v_r.at[i])
        arrived(buf.at[pl.ds(0, count - 1)], v_s.at[i])
        total = buf[0]
        for k in range(1, count):
            total = total + buf[k]
        vec[...] = total

    vec_send(vrz, "z", 0)
    advance(pj + 2)
    advance(pj + 1, *every)
    vec_sum(vrz, "z", 0)
    vec_send(vrx, "lat", 1)
    advance(pj + 2)
    advance(pj + 1, *every)
    vec_sum(vrx, "lat", 1)
    vec_send(vrc, "core", 2)
    advance(pj + 2)
    advance(pj + 1, *every)
    vec_sum(vrc, "core", 2)
    vec_copy = pltpu.make_async_copy(vec, out_vec, in_sem.at[0])
    vec_copy.start()
    for p in range(np_):
        while reached[p] <= last_step[p]:
            advance(p)

    pl.when(has_up)(halo_up.wait_send)
    pl.when(has_down)(halo_dn.wait_send)
    for to_up, to_dn in ((g_up, g_dn), (l_up, l_dn), sent0, sent1):
        pl.when(has_up)(to_up.wait_send)
        pl.when(has_down)(to_dn.wait_send)
    layer_copy.wait()
    patch_copy.wait()
    vec_copy.wait()
    for p in range(np_):
        finish(p)


def widen(plan, *refs):
    pn = plan
    np_ = len(pn.sizes)
    ag, vec, layer, patch = refs[:np_], refs[np_], refs[np_ + 1], refs[np_ + 2]
    o_layer, o_patch, o_ag, o_ab, o_qkv, o_proj, o_mg, o_mb, o_hid, o_out = refs[np_ + 3 : np_ + 13]
    sc = list(refs[np_ + 13 :])
    low, wide = sc[:np_], sc[np_ : 2 * np_]
    kept_layer, kept_patch, in_sem, out_sem, pass_sem = sc[2 * np_ :]
    D = pn.width
    loads = [pltpu.make_async_copy(ag[p], low[p], in_sem.at[p]) for p in range(np_)]
    for c in loads:
        c.start()
    through = [
        (pltpu.make_async_copy(a, b, pass_sem.at[2 * i]), pltpu.make_async_copy(b, c, pass_sem.at[2 * i + 1]))
        for i, (a, b, c) in enumerate(((layer, kept_layer, o_layer), (patch, kept_patch, o_patch)))
    ]
    for arrive, _ in through:
        arrive.start()
    for i, o in enumerate((o_ag, o_ab, o_mg, o_mb)):
        o[...] = vec[i : i + 1, :].reshape(D)
    stores = []

    def store(src, dst):
        c = pltpu.make_async_copy(src, dst, out_sem.at[len(stores)])
        c.start()
        stores.append(c)

    def spread(p, start, rows, blocks, col):
        for j in range(blocks):
            wide[p][:, col + j * 128 : col + (j + 1) * 128] = low[p][
                start + j * rows : start + (j + 1) * rows, :
            ].astype(F32)

    for p in range(np_):
        loads[p].wait()
        if p == np_ - 1:
            for arrive, leave in through:
                arrive.wait()
                leave.start()
        if p < pn.chunks:
            spread(p, 0, CHUNK, D // 128, 0)
            store(wide[p].at[:, pl.ds(0, D)], o_out.at[pl.ds(p * CHUNK, CHUNK)])
            spread(p, CHUNK * (D // 128), D, CHUNK // 128, D)
            store(wide[p].at[:, pl.ds(D, CHUNK)], o_hid.at[:, pl.ds(p * CHUNK, CHUNK)])
        elif p == pn.chunks:
            spread(p, 0, D, D // 128, 0)
            store(wide[p], o_proj)
        else:
            g = p - pn.chunks - 1
            spread(p, 0, D, 3 * WIDE // 128, 0)
            for j in range(3):
                store(
                    wide[p].at[:, pl.ds(j * WIDE, WIDE)],
                    o_qkv.at[:, pl.ds(j * D + g * WIDE, WIDE)],
                )
    for c in stores + [leave for _, leave in through]:
        c.wait()


def per_device(mesh, patches, segment_ids, gain_attn, bias_attn, w_qkv, w_proj, gain_mlp, bias_mlp, w_hidden, w_output, cotangent):
    fields, rows, cols, width = patches.shape
    ff = w_hidden.shape[1]
    pn = Plan(mesh, fields, rows, cols, width, ff)
    np_ = len(pn.sizes)
    T, TF, D, C, R, FD = pn.tokens, pn.tf, width, cols, rows, fields
    L, Z = pn.lats, pn.zs
    anywhere = pl.BlockSpec(memory_space=pl.ANY)
    vmem = pl.BlockSpec(memory_space=pltpu.VMEM)
    V = pltpu.VMEM
    dma = pltpu.SemaphoreType.DMA
    scratch = [
        V((D, 3 * D), BF), V((D, D), BF), V((D, ff), BF), V((ff, D), BF),
        V((FD, TF, D), BF), V((T, D), BF), V(segment_ids.shape, jnp.int32), V((2, FD, C, D), BF),
        V((T, D), BF), V((T, D), BF), V((FD, TF + 2 * C, 2 * D), BF), V((FD, 2 * R, 3 * C, WIDE), BF),
        V((T, D), BF), V((T, D), F32), V((T, D), BF), V((T, D), F32),
        V((T, ff), BF), V((T, ff), BF), V((FD, TF, D), BF), V((2, T, 3 * WIDE), BF),
        V((TF + 2 * C, 2 * WIDE), F32), V((2, 2, FD, C, 2 * WIDE), F32),
        V((2, FD * C, D), BF), V((2, FD, C, D), BF),
        V((2, 2 * FD, WIDE), F32), V((2, 2 * FD, WIDE), F32), V((2, 2, FD, WIDE), F32), V((2, 2, FD, WIDE), F32),
        V((WIDE, WIDE), BF), V((WIDE, WIDE), F32), V((FD, C, WIDE), F32),
        V((8, D), F32), V((Z, 8, D), F32), V((L, 8, D), F32), V((2, 8, D), F32),
    ]
    scratch += [V((n, 128), BF) for n in pn.sizes]
    scratch += [V((n, 128), BF) for n in pn.landing]
    scratch += [V((n, 128), BF) for n in pn.sizes]
    scratch += [
        dma((7,)), dma((2 + np_,)), dma((2,)), dma((2,)), dma((8,)), dma((8,)),
        dma((pn.n_subs, 8)), dma((pn.n_subs, 8)), dma((3,)), dma((3,)),
    ]
    shape = jax.ShapeDtypeStruct
    outs = pl.pallas_call(
        functools.partial(body, pn),
        out_shape=[shape((T, D), BF), shape((T, D), F32), shape((8, D), F32)]
        + [shape((n, 128), BF) for n in pn.sizes],
        in_specs=[anywhere, anywhere, vmem, vmem, anywhere, anywhere, vmem, vmem, anywhere, anywhere, anywhere],
        out_specs=[anywhere] * (3 + np_),
        scratch_shapes=scratch,
        compiler_params=pltpu.CompilerParams(
            collective_id=0, has_side_effects=True, vmem_limit_bytes=62 * 2**20
        ),
        name="block",
    )(
        patches.reshape(FD, TF, D), segment_ids, gain_attn, bias_attn, w_qkv, w_proj, gain_mlp, bias_mlp,
        w_hidden, w_output, cotangent.reshape(T, D),
    )
    layer, patch, vec = outs[:3]
    ags = outs[3:]
    wides = [(D, D + CHUNK)] * pn.chunks + [(D, D)] + [(D, 3 * WIDE)] * 2
    final = pl.pallas_call(
        functools.partial(widen, pn),
        out_shape=[
            shape((T, D), BF), shape((T, D), F32), shape((D,), F32), shape((D,), F32), shape((D, 3 * D), F32),
            shape((D, D), F32), shape((D,), F32), shape((D,), F32), shape((D, ff), F32), shape((ff, D), F32),
        ],
        in_specs=[anywhere] * np_ + [vmem, anywhere, anywhere],
        out_specs=[anywhere, anywhere, vmem, vmem, anywhere, anywhere, vmem, vmem, anywhere, anywhere],
        scratch_shapes=[V((n, 128), BF) for n in pn.sizes]
        + [V(s, F32) for s in wides]
        + [V((T, D), BF), V((T, D), F32), dma((np_,)), dma((2 * pn.chunks + 7,)), dma((4,))],
        compiler_params=pltpu.CompilerParams(vmem_limit_bytes=62 * 2**20),
        name="widen",
    )(*ags, vec, layer, patch)
    block = (FD, R, C, D)
    return (final[0].reshape(block), final[1].reshape(block)) + tuple(final[2:])


def solution(mesh):
    band = P("fld", "lat", None, None)
    return jax.shard_map(
        functools.partial(per_device, mesh),
        mesh=mesh,
        in_specs=(band, P("fld", None, None)) + (P(),) * 8 + (band,),
        out_specs=(band, band) + (P(),) * 8,
        check_vma=False,
    )
```

time: 186 us -> 159 us (0.85); the launches traced: 183 us -> 159 us
  Pallas kernels: 171 us -> 158 us
  local copies, waits for them, and re-layouts: 11.7 us -> 0 us
    pallas_call x1, Pallas kernels: 164 us -> 148 us  [per_device(): pl.pallas_call(functools.partial(body, pn), out_shape=[shape((T, D), BF),...]
    unnamed x20 -> x0, local copies, waits for them, and re-layouts: 11.7 us -> none
    pallas_call x1, Pallas kernels: 6.71 us -> 10.5 us  [per_device(): pl.pallas_call(functools.partial(widen, pn), out_shape=[shape((T, D), BF)...]
where the time goes in v2:
time: 159 us
  Pallas kernels  158 us (99%)
    pallas_call x1, Pallas kernels, per_device(): pl.pallas_call(functools.partial(body, pn), out_shape=[shape((T, D), BF),...  148 us
    pallas_call x1, Pallas kernels, per_device(): pl.pallas_call(functools.partial(widen, pn), out_shape=[shape((T, D), BF)...  10.5 us

profile of v2, /device:TPU:1, one launch (start us, length us, event | category | flops | bytes accessed | tf_op | source)
XLA Modules:
  0.0 158.9 jit_solution(7761991894597114683)
XLA Ops:
  0.6 147.6 %block.1 = (bf16[1024,512]{1,0:T(8,128)(2,1)}, f32[1024,512]{1,0:T(8,128)}, f32[8,512]{1,0:T(8,128)}, bf16[4096,128]{1,0:T(8,128)(2,1)}, bf16[4096,128]{1,0:T(8,...) custom-call(bf16[8,128,512]{2,1,0:T(8,128)(2,1)} %bitcast.4, ...), custom_call_target="tpu_custom_call" | custom-call | tf_op jit(solution)/shard_map/block/pallas_call | solution.py:677
  148.2 10.5 %widen.1 = (bf16[1024,512]{1,0:T(8,128)(2,1)}, f32[1024,512]{1,0:T(8,128)}, f32[512]{0:T(512)}, f32[512]{0:T(512)}, f32[512,1536]{1,0:T(8,128)}, /*index=5*/f32[...) custom-call(bf16[4096,128]{1,0:T(8,128)(2,1)} %get-tuple-element.30.refs_0_, ...), custom_call_target="tpu_custom_call" | custom-call | tf_op jit(solution)/shard_map/widen/pallas_call | solution.py:695

commit v3 on v2

--- a/solution.py
+++ b/solution.py
@@ -17,6 +17,15 @@
 REACH = 4
 NEG = -1e30
 CHUNK = 512
+BLOCK = 256
+FIELDS_AT_ONCE = 2
+SCHEDULE = {
+    "J2": (0,), "J4": (0, 1), "J6": (2,), "J7": (1,), "J8": (3, 0),
+    "E0": (2,), "E1": (1,), "E2": (3,), "E3": (), "P": (0,), "P1": (4, 2),
+    "A0": (1,), "A1": (4, 3), "A2": (0,), "A3": (2, 1),
+    "B0": (4, 3), "B1": (0,), "B2": (2, 1), "B3": (5, 3, 4),
+    "C0": (0, 5, 2), "C1": (6, 1, 3, 4), "D0": (0, 6, 2), "D1": (5, 1), "D2": (3, 4), "D3": (0, 2),
+}
 BF = jnp.bfloat16
 F32 = jnp.float32
 MESH = pl.DeviceIdType.MESH
@@ -46,13 +55,9 @@
 
 
 def gelu_both(u):
-    z = jnp.abs(u) * (1.0 / math.sqrt(2.0))
-    t = 1.0 / (1.0 + 0.3275911 * z)
-    ex = jnp.exp2((u * u) * (-0.5 * LOG2E))
-    poly = t * (0.254829592 + t * (-0.284496736 + t * (1.421413741 + t * (-1.453152027 + t * 1.061405429))))
-    half = 0.5 * poly * ex
-    cdf = jnp.where(u < 0, half, 1.0 - half)
-    return u * cdf, cdf + u * (ex * (1.0 / math.sqrt(2.0 * math.pi)))
+    cdf = 0.5 + 0.5 * lax.erf(u * (1.0 / math.sqrt(2.0)))
+    density = jnp.exp2((u * u) * (-0.5 * LOG2E)) * (1.0 / math.sqrt(2.0 * math.pi))
+    return u * cdf, cdf + u * density
 
 
 def row_sums(x):
@@ -109,9 +114,9 @@
 
     wq, wp, wh, wo = take(4)
     pb, cb, segv, halo = take(4)
-    normed, qb, kv, pt, ctx, res, nm, gres, act, gpre, gctx, dq, dacc, edge = take(14)
+    normed, qb, kv, pt, ctx, res, nm, gres, act, gpre, gctx, edge = take(12)
     hq, hg, lse, hlse, dst, hdst = take(6)
-    bm, bmf, biasb, vec, vrz, vrx, vrc = take(7)
+    bm, biasb, vec, vrz, vrx, vrc = take(6)
     sb, rb, ag = take(np_), take(np_), take(np_)
     in_sem, out_sem, halo_s, halo_r, back_s, back_r, rs_s, rs_r, v_s, v_r = take(10)
 
@@ -261,41 +266,52 @@
 
         return run
 
-    def advance(*pieces):
-        hook(*pieces)()
+    def place(name):
+        return hook(*SCHEDULE.get(name, ()))
 
     def finish(p):
         for part in parts[p]:
             part.finish()
         pltpu.make_async_copy(ag[p], out_ag[p], out_sem.at[2 + p]).wait()
 
-    def put(p, start, value):
+    def put(p, start, stride, value):
         rows, lanes = value.shape
         low = value.astype(BF)
         for j in range(lanes // 128):
-            sb[p][start + j * rows : start + (j + 1) * rows, :] = low[:, j * 128 : (j + 1) * 128]
+            at = start + j * stride
+            sb[p][at : at + rows, :] = low[:, j * 128 : (j + 1) * 128]
 
     rid = lax.broadcasted_iota(jnp.int32, (WIDE, WIDE), 0) // HEAD_DIM
     cid = lax.broadcasted_iota(jnp.int32, (WIDE, WIDE), 1) // HEAD_DIM
     same = jnp.where(rid == cid, 1.0, 0.0)
     bm[...] = same.astype(BF)
-    bmf[...] = same
 
     ga, ba = gain_a[...].reshape(1, D), bias_a[...].reshape(1, D)
     gm, bmlp = gain_m[...].reshape(1, D), bias_m[...].reshape(1, D)
     loads[0].wait()
 
-    def norm_one(f, carry):
-        n, _ = normalize(pb[f].astype(F32))
-        normed[pl.ds(pl.multiple_of(f * TF, TF), TF), :] = (n * ga + ba).astype(BF)
-        return carry
-
-    lax.fori_loop(0, FD, norm_one, 0)
+    per = max(1, 256 // TF)
+    tile = per * TF
+    tiles = T // tile
+
+    def rows_at(t):
+        return slice(t * tile, (t + 1) * tile)
+
+    def fields_at(t):
+        return slice(t * per, (t + 1) * per)
+
+    def norm_one(t):
+        n, _ = normalize(pb[fields_at(t)].reshape(tile, D).astype(F32))
+        normed[rows_at(t), :] = (n * ga + ba).astype(BF)
+
+    norm_one(0)
     loads[1].wait()
-    qb[...] = dot(normed[...], wq[:, :D]).astype(BF)
-    for j in range(2):
-        part = dot(normed[...], wq[:, (j + 1) * D : (j + 2) * D]).astype(BF)
-        kv[:, C : C + TF, j * D : (j + 1) * D] = part.reshape(FD, TF, D)
+    for t in range(tiles):
+        if t + 1 < tiles:
+            norm_one(t + 1)
+        qb[rows_at(t), :] = dot(normed[rows_at(t), :], wq[:, :D]).astype(BF)
+        part = dot(normed[rows_at(t), :], wq[:, D:]).astype(BF)
+        kv[fields_at(t), C : C + TF, :] = part.reshape(per, TF, 2 * D)
 
     loads[2].wait()
     kcol = lax.broadcasted_iota(jnp.int32, (C, WIDE), 0)
@@ -311,40 +327,55 @@
     pole_top = jnp.where(has_up, 0.0, NEG)
     pole_bottom = jnp.where(has_down, 0.0, NEG)
 
+    lane_head = lax.broadcasted_iota(jnp.int32, (HEAD_DIM, WIDE), 1) // HEAD_DIM
+
     def diagonal(o):
-        o = o * bmf[...]
         total = o[0:HEAD_DIM]
         for h in range(1, GROUP):
-            total = total + o[h * HEAD_DIM : (h + 1) * HEAD_DIM]
+            total = jnp.where(lane_head == h, o[h * HEAD_DIM : (h + 1) * HEAD_DIM], total)
         return total
 
     def widened(q):
         return jnp.concatenate([q] * GROUP, axis=0) * bm[...]
 
-    def attend(rows, f, carry):
-        bias = biasb[f]
-        for g in range(2):
-            lanes = slice(g * WIDE, (g + 1) * WIDE)
-            vlanes = slice(D + g * WIDE, D + (g + 1) * WIDE)
-            for r in rows:
-                tok = pl.ds(pl.multiple_of(f * TF + r * C, C), C)
-                win = slice(r * C, (r + 3) * C)
-                s = dot(kv[f, win, lanes], widened(qb[tok, lanes]), NT)
-                top = bias + pole_top if r == 0 else bias
-                low = bias + pole_bottom if r == R - 1 else bias
-                s = s + jnp.concatenate([top, bias, low], axis=0)
-                m = jnp.max(s, axis=0, keepdims=True)
-                p = jnp.exp2((s - m) * (SCALE * LOG2E))
-                total = row_sums(p)
-                if r == 0 or r == R - 1:
-                    lse[0 if r == 0 else 1, pl.ds(f * 2 + g, 1), :] = m * (SCALE * LOG2E) + jnp.log2(total)
-                p = (p * (1.0 / total)).astype(BF)
-                pt[f, g * R + r] = p
-                ctx[tok, lanes] = diagonal(dot(p, kv[f, win, vlanes], TN)).astype(BF)
+    fpi = min(FIELDS_AT_ONCE, FD)
+
+    def span(f, row):
+        return pl.ds(pl.multiple_of(f * TF + row * C, C), C)
+
+    k_lanes = [slice(g * WIDE, (g + 1) * WIDE) for g in range(2)]
+    v_lanes = [slice(D + g * WIDE, D + (g + 1) * WIDE) for g in range(2)]
+
+    def attend(rows, i, carry):
+        units = [(i * fpi + j, g, r) for j in range(fpi) for g in range(2) for r in rows]
+        scores = []
+        for f, g, r in units:
+            k = kv[f, r * C : (r + 3) * C, k_lanes[g]]
+            scores.append(dot(k, widened(qb[span(f, r), k_lanes[g]]), NT))
+        low, logs = [], []
+        for (f, g, r), s in zip(units, scores):
+            bias = biasb[f]
+            first = bias + pole_top if r == 0 else bias
+            third = bias + pole_bottom if r == R - 1 else bias
+            s = s + jnp.concatenate([first, bias, third], axis=0)
+            m = jnp.max(s, axis=0, keepdims=True)
+            p = jnp.exp2((s - m) * (SCALE * LOG2E))
+            total = row_sums(p)
+            logs.append(m * (SCALE * LOG2E) + jnp.log2(total) if r in (0, R - 1) else None)
+            low.append((p * (1.0 / total)).astype(BF))
+        outs = []
+        for (f, g, r), p in zip(units, low):
+            v = kv[f, r * C : (r + 3) * C, v_lanes[g]]
+            outs.append(diagonal(dot(p, v, TN)).astype(BF))
+        for (f, g, r), p, log, o in zip(units, low, logs, outs):
+            pt[f, g * R + r] = p
+            ctx[span(f, r), k_lanes[g]] = o
+            if r in (0, R - 1):
+                lse[0 if r == 0 else 1, pl.ds(f * 2 + g, 1), :] = log
         return carry
 
     if R > 2:
-        lax.fori_loop(0, FD, functools.partial(attend, range(1, R - 1)), 0)
+        lax.fori_loop(0, FD // fpi, functools.partial(attend, range(1, R - 1)), 0)
 
     for side, ok, copy in ((0, has_up, halo_dn), (1, has_down, halo_up)):
         pl.when(ok)(copy.wait_recv)
@@ -360,62 +391,69 @@
         start = 0 if side == 0 else TF + C
         kv[:, start : start + C, :] = edge_kv
 
-    lax.fori_loop(0, FD, functools.partial(attend, (0, R - 1)), 0)
+    lax.fori_loop(0, FD // fpi, functools.partial(attend, (0, R - 1)), 0)
 
     loads[3].wait()
-    per = max(1, 256 // TF)
-    tile = per * TF
-
-    def project(t, carry):
-        tok = pl.ds(pl.multiple_of(t * tile, tile), tile)
-        r = pb[pl.ds(t * per, per)].reshape(tile, D).astype(F32) + dot(ctx[tok, :], wp[...])
-        res[tok, :] = r
+    for t in range(tiles):
+        r = pb[fields_at(t)].reshape(tile, D).astype(F32) + dot(ctx[rows_at(t), :], wp[...])
+        res[rows_at(t), :] = r
         n, _ = normalize(r)
-        nm[tok, :] = (n * gm + bmlp).astype(BF)
-        return carry
-
-    lax.fori_loop(0, T // tile, project, 0)
+        nm[rows_at(t), :] = (n * gm + bmlp).astype(BF)
 
     for i in (4, 5, 6):
         loads[i].wait()
-    mid = (T // tile) // 2
-    mids = [(), (0,), (0, 1), (0, 1, 2)]
-    ends = [(0,), (1,), (0, 2), (0, 1, 3)]
-    for c in range(pn.chunks):
-        cs = slice(c * CHUNK, (c + 1) * CHUNK)
-
-        meanwhile = hook(*mids[c])
-
-        def mlp_tile(t, carry, cs=cs, meanwhile=meanwhile):
-            pl.when(t == mid)(meanwhile)
-            tok = pl.ds(pl.multiple_of(t * tile, tile), tile)
-            hidden = dot(nm[tok, :], wh[:, cs])
-            back = dot(cb[tok, :], wo[cs, :], NT)
-            a, da = gelu_both(hidden)
-            act[tok, cs] = a.astype(BF)
-            gpre[tok, cs] = (da * back).astype(BF)
-            return carry
-
-        lax.fori_loop(0, T // tile, mlp_tile, 0)
-        put(c, 0, dot(act[:, cs], cb[...], TN))
-        put(c, CHUNK * (D // 128), dot(nm[...], gpre[:, cs], TN))
-        advance(*ends[c])
+    blocks = FF // BLOCK
+    in_chunk = CHUNK // BLOCK
+
+    def hidden_block(j):
+        return slice(j * BLOCK, (j + 1) * BLOCK)
+
+    def kept(ref, j):
+        return ref.at[pl.ds(0, T), pl.ds((j % 2) * BLOCK, BLOCK)]
+
+    def mlp_in(j):
+        kept(gres, j)[...] = dot(nm[...], wh[:, hidden_block(j)])
+        kept(edge, j)[...] = dot(cb[...], wo[hidden_block(j), :], NT)
+
+    def mlp_mid(j):
+        a, da = gelu_both(kept(gres, j)[...])
+        act[:, hidden_block(j)] = a.astype(BF)
+        gpre[:, hidden_block(j)] = (da * kept(edge, j)[...]).astype(BF)
+
+    def mlp_out(j):
+        c, part = j // in_chunk, j % in_chunk
+        put(c, part * BLOCK, CHUNK, dot(act[:, hidden_block(j)], cb[...], TN))
+        start = CHUNK * (D // 128) + part * (BLOCK // 128) * D
+        put(c, start, D, dot(nm[...], gpre[:, hidden_block(j)], TN))
+
+    mlp_in(0)
+    for j in range(blocks):
+        if j + 1 < blocks:
+            mlp_in(j + 1)
+        mlp_mid(j)
+        if j > 0:
+            mlp_out(j - 1)
+        place(f"J{j}")()
+    mlp_out(blocks - 1)
+    place(f"J{blocks}")()
 
     zero = jnp.zeros((1, D), F32)
 
-    def mlp_end(t, carry):
-        dg, db = carry
-        tok = pl.ds(pl.multiple_of(t * tile, tile), tile)
-        e = dot(gpre[tok, :], wh[...], NT)
-        n, rstd = normalize(res[tok, :])
-        gr = cb[tok, :].astype(F32) + norm_pull(e, gm, n, rstd)
-        gres[tok, :] = gr
+    mlp_gain, mlp_bias = zero, zero
+    grad_in = dot(gpre[rows_at(0), :], wh[...], NT)
+    for t in range(tiles):
+        e = grad_in
+        if t + 1 < tiles:
+            grad_in = dot(gpre[rows_at(t + 1), :], wh[...], NT)
+        n, rstd = normalize(res[rows_at(t), :])
+        gr = cb[rows_at(t), :].astype(F32) + norm_pull(e, gm, n, rstd)
+        gres[rows_at(t), :] = gr
         low = gr.astype(BF)
-        nm[tok, :] = low
-        gctx[pl.ds(t * per, per)] = dot(low, wp[...], NT).astype(BF).reshape(per, TF, D)
-        return dg + row_sums(e * n), db + row_sums(e)
-
-    mlp_gain, mlp_bias = lax.fori_loop(0, T // tile, mlp_end, (zero, zero))
+        nm[rows_at(t), :] = low
+        gctx[fields_at(t)] = dot(low, wp[...], NT).astype(BF).reshape(per, TF, D)
+        mlp_gain, mlp_bias = mlp_gain + row_sums(e * n), mlp_bias + row_sums(e)
+        place(f"E{t}")()
+
     pj = pn.chunks
     g_up = remote(gctx.at[:, pl.ds(0, C)], hg.at[1], back_s.at[0], back_r.at[1], up)
     g_dn = remote(gctx.at[:, pl.ds(TF - C, C)], hg.at[0], back_s.at[1], back_r.at[0], down)
@@ -424,118 +462,147 @@
     for to_up, to_dn in ((g_up, g_dn), (l_up, l_dn)):
         pl.when(has_up)(to_up.start)
         pl.when(has_down)(to_dn.start)
-    advance(1, 2)
-    put(pj, 0, dot(ctx[...], nm[...], TN))
-    advance(0, 3, pj)
+    place("P")()
+    put(pj, 0, D, dot(ctx[...], nm[...], TN))
+    place("P1")()
+
+    grad_joined = gpre
+
+    def joined(g, j):
+        return slice((3 * g + j) * WIDE, (3 * g + j + 1) * WIDE)
+
+    def edge_rows(g, side, f):
+        return pl.ds(pl.multiple_of(((g * 2 + side) * FD + f) * C, C), C)
 
     def back_group(g, hooks):
-        lanes = slice(g * WIDE, (g + 1) * WIDE)
-        vlanes = slice(D + g * WIDE, D + (g + 1) * WIDE)
-
-        def back_field(f, carry):
+        def back_fields(i, carry):
             for when, do in hooks.items():
-                pl.when(f == when)(do)
-            dacc[...] = jnp.zeros_like(dacc)
-            for r in range(R):
-                tok = pl.ds(pl.multiple_of(f * TF + r * C, C), C)
+                pl.when(i == when)(do)
+            units = [(i * fpi + j, r) for j in range(fpi) for r in range(R)]
+            have = []
+            for f, r in units:
                 win = slice(r * C, (r + 3) * C)
-                qd = widened(qb[tok, lanes])
-                dod = widened(gctx[f, r * C : (r + 1) * C, lanes])
-                k = kv[f, win, lanes]
-                p = pt[f, g * R + r]
-                dp = dot(kv[f, win, vlanes], dod, NT)
+                qd = widened(qb[span(f, r), k_lanes[g]])
+                dod = widened(gctx[f, r * C : (r + 1) * C, k_lanes[g]])
+                have.append((qd, dod, kv[f, win, k_lanes[g]], kv[f, win, v_lanes[g]], pt[f, g * R + r]))
+            dps = [dot(v, dod, NT) for qd, dod, k, v, p in have]
+            dss, totals = [], []
+            for (qd, dod, k, v, p), dp in zip(have, dps):
                 wide = p.astype(F32)
                 pd = wide * dp
                 total = row_sums(pd)
-                if r == 0 or r == R - 1:
+                totals.append(total)
+                dss.append(((pd - wide * total) * SCALE).astype(BF))
+            dqs = [diagonal(dot(ds, one[2], TN)).astype(BF) for ds, one in zip(dss, have)]
+            dks, dvs = [], []
+            for (f, r), ds, (qd, dod, k, v, p) in zip(units, dss, have):
+                own = slice(C if r == 0 else 0, 2 * C if r == R - 1 else 3 * C)
+                first = r + 1 if r == 0 else r
+                dks.append((first, dot(ds[own], qd)))
+                dvs.append((first, dot(p[own], dod)))
+            for (f, r), o, total in zip(units, dqs, totals):
+                grad_joined[span(f, r), joined(g, 0)] = o
+                if r in (0, R - 1):
                     dst[g, 0 if r == 0 else 1, pl.ds(f, 1), :] = total
-                ds = ((pd - wide * total) * SCALE).astype(BF)
-                dq[g, tok, 0:WIDE] = diagonal(dot(ds, k, TN)).astype(BF)
-                dacc[win, 0:WIDE] += dot(ds, qd)
-                dacc[win, WIDE:] += dot(p, dod)
-            edge[g, 0, f] = dacc[C : 2 * C, :]
-            edge[g, 1, f] = dacc[TF : TF + C, :]
-            if R > 2:
-                inner = pl.ds(pl.multiple_of(f * TF + C, C), TF - 2 * C)
-                dq[g, inner, WIDE:] = dacc[2 * C : TF, :].astype(BF)
+            for j in range(fpi):
+                f = i * fpi + j
+                for what, terms in enumerate((dks, dvs)):
+                    for row in range(1, R + 1):
+                        total = None
+                        for first, term in terms[j * R : (j + 1) * R]:
+                            if first <= row < first + term.shape[0] // C:
+                                piece = term[(row - first) * C : (row - first + 1) * C]
+                                total = piece if total is None else total + piece
+                        if row in (1, R):
+                            edge[edge_rows(g, 0 if row == 1 else 1, f), what * WIDE : (what + 1) * WIDE] = total
+                        else:
+                            grad_joined[span(f, row - 1), joined(g, what + 1)] = total.astype(BF)
             return carry
 
-        lax.fori_loop(0, FD, back_field, 0)
+        lax.fori_loop(0, FD // fpi, back_fields, 0)
         to_up = remote(dst.at[g, 0], hdst.at[g, 1], back_s.at[4 + 2 * g], back_r.at[5 + 2 * g], up)
         to_dn = remote(dst.at[g, 1], hdst.at[g, 0], back_s.at[5 + 2 * g], back_r.at[4 + 2 * g], down)
         pl.when(has_up)(to_up.start)
         pl.when(has_down)(to_dn.start)
         return to_up, to_dn
 
+    fpe = min(2 * FIELDS_AT_ONCE, FD)
+
     def back_edges(g, sent):
-        lanes = slice(g * WIDE, (g + 1) * WIDE)
-        vlanes = slice(D + g * WIDE, D + (g + 1) * WIDE)
         for to_up, to_dn in sent:
             pl.when(has_up)(to_dn.wait_recv)
             pl.when(has_down)(to_up.wait_recv)
 
-        def one(f, carry):
-            for side, ok, row in ((0, has_up, 0), (1, has_down, R - 1)):
-                tok = pl.ds(pl.multiple_of(f * TF + row * C, C), C)
-                keys = slice((row + 1) * C, (row + 2) * C)
-                qd = widened(hq[side, pl.ds(pl.multiple_of(f * C, C), C), lanes])
-                dod = widened(hg[side, f, :, lanes])
-                s = dot(kv[f, keys, lanes], qd, NT) + biasb[f]
-                p = jnp.exp2(s * (SCALE * LOG2E) - hlse[side, pl.ds(f * 2 + g, 1), :])
-                p = jnp.where(ok, p, 0.0)
-                dp = dot(kv[f, keys, vlanes], dod, NT)
+        def back_rims(i, carry):
+            units = [(i * fpe + j, side) for j in range(fpe) for side in range(2)]
+            oks, rows = (has_up, has_down), (0, R - 1)
+            have = []
+            for f, side in units:
+                qd = widened(hq[side, pl.ds(pl.multiple_of(f * C, C), C), k_lanes[g]])
+                dod = widened(hg[side, f, :, k_lanes[g]])
+                keys = slice((rows[side] + 1) * C, (rows[side] + 2) * C)
+                have.append((qd, dod, kv[f, keys, k_lanes[g]], kv[f, keys, v_lanes[g]]))
+            scores = [dot(k, qd, NT) for qd, dod, k, v in have]
+            dps = [dot(v, dod, NT) for qd, dod, k, v in have]
+            ps, dss = [], []
+            for (f, side), s, dp in zip(units, scores, dps):
+                s = (s + biasb[f]) * (SCALE * LOG2E) - hlse[side, pl.ds(f * 2 + g, 1), :]
+                p = jnp.where(oks[side], jnp.exp2(s), 0.0)
                 ds = p * (dp - hdst[g, side, pl.ds(f, 1), :]) * SCALE
-                ds = jnp.where(ok, ds, 0.0).astype(BF)
-                dk = edge[g, side, f, :, 0:WIDE] + jnp.where(ok, dot(ds, qd), 0.0)
-                dv = edge[g, side, f, :, WIDE:] + jnp.where(ok, dot(p.astype(BF), dod), 0.0)
-                dq[g, tok, WIDE : 2 * WIDE] = dk.astype(BF)
-                dq[g, tok, 2 * WIDE :] = dv.astype(BF)
+                ps.append(p.astype(BF))
+                dss.append(jnp.where(oks[side], ds, 0.0).astype(BF))
+            dks = [dot(ds, one[0]) for ds, one in zip(dss, have)]
+            dvs = [dot(p, one[1]) for p, one in zip(ps, have)]
+            held = [edge[edge_rows(g, side, f), :] for f, side in units]
+            for (f, side), dk, dv, own in zip(units, dks, dvs, held):
+                dk = own[:, :WIDE] + jnp.where(oks[side], dk, 0.0)
+                dv = own[:, WIDE:] + jnp.where(oks[side], dv, 0.0)
+                grad_joined[span(f, rows[side]), joined(g, 1)] = dk.astype(BF)
+                grad_joined[span(f, rows[side]), joined(g, 2)] = dv.astype(BF)
             return carry
 
-        lax.fori_loop(0, FD, one, 0)
-        put(pj + 1 + g, 0, dot(normed[...], dq[g], TN))
-
-    every = list(range(pj + 1))
-    sent0 = back_group(0, {1: hook(1, 2), 3: hook(0, 3, pj), 5: hook(1, 2), 7: hook(0, 3, pj)})
-
-    early = {0: hook(1, 2), 2: hook(0, 3, pj)}
-    start_first = hook(pj + 1)
+        lax.fori_loop(0, FD // fpe, back_rims, 0)
+        put(pj + 1 + g, 0, D, dot(normed[...], grad_joined[:, 3 * g * WIDE : 3 * (g + 1) * WIDE], TN))
+
+    sent0 = back_group(0, {i: place(f"A{i}") for i in range(4)})
+    early = {i: place(f"B{i}") for i in range(2)}
+    later = {i: place(f"B{i}") for i in range(2, 4)}
+    about = later[3]
 
     def first_edges():
+        later[2]()
         back_edges(0, ((g_up, g_dn), (l_up, l_dn), sent0))
-        start_first()
-
-    sent1 = back_group(1, early | {4: first_edges, 5: hook(1, 2, pj + 1), 6: hook(3, pj), 7: hook(2, pj)})
-    advance(3, pj + 1)
+
+    sent1 = back_group(1, early | {2: first_edges, 3: about})
+    place("C0")()
     back_edges(1, (sent1,))
-    advance(pj + 2)
-    advance(pj + 1, *every)
-
-    def out_tile(t, carry):
-        tok = pl.ds(pl.multiple_of(t * tile, tile), tile)
-        nm[tok, :] = (res[tok, :] + dot(act[tok, :], wo[...])).astype(BF)
-        return carry
-
-    lax.fori_loop(0, T // tile, out_tile, 0)
+    place("C1")()
+
+    for t in range(tiles):
+        nm[rows_at(t), :] = (res[rows_at(t), :] + dot(act[rows_at(t), :], wo[...])).astype(BF)
     layer_copy = pltpu.make_async_copy(nm, out_layer, out_sem.at[0])
     layer_copy.start()
-    advance(pj + 2)
-    advance(pj + 1, *every)
-
-    def last_tile(t, carry):
-        dg, db = carry
-        tok = pl.ds(pl.multiple_of(t * tile, tile), tile)
+    place("D0")()
+    attn_gain, attn_bias = zero, zero
+
+    def grad_of(t):
         e = None
         for g in range(2):
             for j in range(3):
                 w = wq[:, j * D + g * WIDE : j * D + (g + 1) * WIDE]
-                term = dot(dq[g, tok, j * WIDE : (j + 1) * WIDE], w, NT)
+                term = dot(grad_joined[rows_at(t), joined(g, j)], w, NT)
                 e = term if e is None else e + term
-        n, rstd = normalize(pb[pl.ds(t * per, per)].reshape(tile, D).astype(F32))
-        gres[tok, :] += norm_pull(e, ga, n, rstd)
-        return dg + row_sums(e * n), db + row_sums(e)
-
-    attn_gain, attn_bias = lax.fori_loop(0, T // tile, last_tile, (zero, zero))
+        return e
+
+    grad_in = grad_of(0)
+    for t in range(tiles):
+        e = grad_in
+        if t + 1 < tiles:
+            grad_in = grad_of(t + 1)
+        n, rstd = normalize(pb[fields_at(t)].reshape(tile, D).astype(F32))
+        gres[rows_at(t), :] += norm_pull(e, ga, n, rstd)
+        attn_gain, attn_bias = attn_gain + row_sums(e * n), attn_bias + row_sums(e)
+
     patch_copy = pltpu.make_async_copy(gres, out_patch, out_sem.at[1])
     patch_copy.start()
     vec[...] = jnp.concatenate([attn_gain, attn_bias, mlp_gain, mlp_bias, zero, zero, zero, zero], axis=0)
@@ -555,22 +622,19 @@
         vec[...] = total
 
     vec_send(vrz, "z", 0)
-    advance(pj + 2)
-    advance(pj + 1, *every)
+    place("D1")()
     vec_sum(vrz, "z", 0)
     vec_send(vrx, "lat", 1)
-    advance(pj + 2)
-    advance(pj + 1, *every)
+    place("D2")()
     vec_sum(vrx, "lat", 1)
     vec_send(vrc, "core", 2)
-    advance(pj + 2)
-    advance(pj + 1, *every)
+    place("D3")()
     vec_sum(vrc, "core", 2)
     vec_copy = pltpu.make_async_copy(vec, out_vec, in_sem.at[0])
     vec_copy.start()
-    for p in range(np_):
-        while reached[p] <= last_step[p]:
-            advance(p)
+    while any(reached[p] <= last_step[p] for p in range(np_)):
+        for p in sorted(range(np_), key=lambda p: reached[p] - last_step[p], reverse=True):
+            hook(p)()
 
     pl.when(has_up)(halo_up.wait_send)
     pl.when(has_down)(halo_dn.wait_send)
@@ -659,11 +723,11 @@
         V((FD, TF, D), BF), V((T, D), BF), V(segment_ids.shape, jnp.int32), V((2, FD, C, D), BF),
         V((T, D), BF), V((T, D), BF), V((FD, TF + 2 * C, 2 * D), BF), V((FD, 2 * R, 3 * C, WIDE), BF),
         V((T, D), BF), V((T, D), F32), V((T, D), BF), V((T, D), F32),
-        V((T, ff), BF), V((T, ff), BF), V((FD, TF, D), BF), V((2, T, 3 * WIDE), BF),
-        V((TF + 2 * C, 2 * WIDE), F32), V((2, 2, FD, C, 2 * WIDE), F32),
+        V((T, ff), BF), V((T, ff), BF), V((FD, TF, D), BF),
+        V((max(4 * FD * C, T), 2 * WIDE), F32),
         V((2, FD * C, D), BF), V((2, FD, C, D), BF),
         V((2, 2 * FD, WIDE), F32), V((2, 2 * FD, WIDE), F32), V((2, 2, FD, WIDE), F32), V((2, 2, FD, WIDE), F32),
-        V((WIDE, WIDE), BF), V((WIDE, WIDE), F32), V((FD, C, WIDE), F32),
+        V((WIDE, WIDE), BF), V((FD, C, WIDE), F32),
         V((8, D), F32), V((Z, 8, D), F32), V((L, 8, D), F32), V((2, 8, D), F32),
     ]
     scratch += [V((n, 128), BF) for n in pn.sizes]

time: 159 us -> 132 us (0.83)
  Pallas kernels: 158 us -> 131 us
    pallas_call x1, Pallas kernels: 148 us -> 120 us  [per_device(): pl.pallas_call(functools.partial(body, pn), out_shape=[shape((T, D), BF),...]
where the time goes in v3:
time: 132 us
  Pallas kernels  131 us (99%)
    pallas_call x1, Pallas kernels, per_device(): pl.pallas_call(functools.partial(body, pn), out_shape=[shape((T, D), BF),...  120 us
    pallas_call x1, Pallas kernels, per_device(): pl.pallas_call(functools.partial(widen, pn), out_shape=[shape((T, D), BF)...  10.5 us

profile of v3, /device:TPU:1, one launch (start us, length us, event | category | flops | bytes accessed | tf_op | source)
XLA Modules:
  0.0 131.6 jit_solution(551858126072348304)
XLA Ops:
  0.6 120.2 %block.1 = (bf16[1024,512]{1,0:T(8,128)(2,1)}, f32[1024,512]{1,0:T(8,128)}, f32[8,512]{1,0:T(8,128)}, bf16[4096,128]{1,0:T(8,128)(2,1)}, bf16[4096,128]{1,0:T(8,...) custom-call(bf16[8,128,512]{2,1,0:T(8,128)(2,1)} %bitcast.4, ...), custom_call_target="tpu_custom_call" | custom-call | tf_op jit(solution)/shard_map/block/pallas_call | solution.py:741
  120.9 10.5 %widen.1 = (bf16[1024,512]{1,0:T(8,128)(2,1)}, f32[1024,512]{1,0:T(8,128)}, f32[512]{0:T(512)}, f32[512]{0:T(512)}, f32[512,1536]{1,0:T(8,128)}, /*index=5*/f32[...) custom-call(bf16[4096,128]{1,0:T(8,128)(2,1)} %get-tuple-element.30.refs_0_, ...), custom_call_target="tpu_custom_call" | custom-call | tf_op jit(solution)/shard_map/widen/pallas_call | solution.py:759
